TPU v7x, 32 devices: a whole 2x2x4 slice. The times are simulated.
32 devices in a mesh: ens: 2 (over x), tile: 8 (over z, y), lev: 2 (over core).
Axes of the slice: x: 2, y: 2, z: 4, core: 2. Of those that a mesh axis runs over, the one named last changes fastest.
Arguments:
- cotangent: float32 [34, 5, 8, 4, 18432], P(None, None, 'lev', None, ('ens', 'tile')), parts along dimension 4, may hold values from -6 to 6
- stencil_col: int32 [5, 18432], P(None, ('ens', 'tile')), parts along dimension 1, may hold values from 0 to 3071, as said below
- stencil_row: int32 [5, 18432], P(None, ('ens', 'tile')), parts along dimension 1, may hold values from 0 to 2, as said below
- frac_along: float32 [5, 18432], P(None, ('ens', 'tile')), parts along dimension 1, may hold values from 0 to 1
- frac_across: float32 [5, 18432], P(None, ('ens', 'tile')), parts along dimension 1, may hold values from 0 to 1
- owner_map: int32 [16, 8], P(('ens', 'tile')), parts along dimension 0, may hold values from 0 to 7, as said below
Outputs:
- parent_grad: float32 [12, 5, 8, 6, 6144], P(None, None, 'lev', None, ('ens', 'tile')), parts along dimension 4
There are 2 independent parts, one for each index of `ens`. A program takes and returns all parts, laid end to end along the dimension named above; each array names one. Nothing has to cross between parts.
Inputs may be any that keep to these rules, and one draw needn't show every extreme that they name: stencil_col[r, p] - p // 3 is -2, -1 or 0 modulo 3072. stencil_row[r, p] - r // 3 is 0 or 1. `owner_map`: every row is a permutation of 0 to 7.
All inputs are finite; a program needn't handle non-finite values.
Results may differ from a plain program's by a relative error of at most 0.00007.
Values sent between devices are 32-bit elements; how exact they have to be, the bound alone decides.
No kernel may reach another device: no remote copies, remote signals or barrier semaphores. Data moves between devices by JAX's collectives and lax.ppermute only.
A program may use at most 448 MiB of HBM per device.

v0:
```python
import functools

import jax
import jax.numpy as jnp
from jax import lax
from jax.experimental import pallas as pl
from jax.experimental.pallas import tpu as pltpu
from jax.sharding import PartitionSpec as P

PROWS = 6
NT = 12
STEPS_PER = 3
LANES = 128
TAPS = 4
SPILL = 4
SPILL_ROWS = 32
EDGE_ROWS = 40
FAR = -(1 << 20)
VMEM_BYTES = 53 << 20
BLOCK_VMEM = 32 << 20


def zone_factors(forced):
    relax = [0.0] + [(forced - r) / (forced - 1.0) for r in range(1, forced)]
    diffuse = [0.2 * value for value in relax]
    center = [1.0] + [relax[r] + 4.0 * diffuse[r] for r in range(1, forced)]
    return center, diffuse


def lagrange_weights(fraction):
    shifted = fraction + 1.0
    return [
        -fraction * (fraction - 1.0) * (fraction - 2.0) / 6.0,
        shifted * (fraction - 1.0) * (fraction - 2.0) / 2.0,
        -shifted * fraction * (fraction - 2.0) / 2.0,
        shifted * fraction * (fraction - 1.0) / 6.0,
    ]


def split_bf16(value):
    high = value.astype(jnp.bfloat16)
    low = (value - high.astype(jnp.float32)).astype(jnp.bfloat16)
    return high, low


def tap_select(distance, weights):
    picked = jnp.where(distance == TAPS - 1, weights[TAPS - 1], 0.0)
    for tap in range(TAPS - 2, -1, -1):
        picked = jnp.where(distance == tap, weights[tap], picked)
    return picked


def first_columns(cols, third, tile_start, total):
    offset = cols - (tile_start + third)
    offset = jnp.where(offset < -2, offset + total, offset)
    offset = jnp.where(offset > 0, offset - total, offset)
    return third + offset


def divided_by_3(value):
    return (value * 21846) >> 16


def diffused_terms(row, forced, center, diffuse):
    terms = [(row, 0, center[row])]
    if diffuse[row] != 0.0:
        terms += [(row, -1, -diffuse[row]), (row, 1, -diffuse[row])]
        terms += [(row + 1, 0, -diffuse[row]), (row - 1, 0, -diffuse[row])]
    return terms


def fold_times(read, write, steps):
    values = {}

    def value(t):
        if t not in values:
            values[t] = read(t)
        return values[t]

    for k in range(NT):
        total = value(STEPS_PER * k)
        for gap in range(1, STEPS_PER):
            near = [value(t) for t in (STEPS_PER * k - gap, STEPS_PER * k + gap) if 0 <= t < steps]
            total = total + (1.0 - gap / STEPS_PER) * functools.reduce(jnp.add, near)
        write(k, total)


class Sizes:
    def __init__(self, cotangent_shape, tile_count):
        self.steps, self.fields, self.levels, self.forced, self.seg = cotangent_shape
        self.tiles = tile_count
        self.par = self.seg // 3
        self.total = self.par * tile_count
        self.bw = self.par // tile_count
        self.each = NT * self.levels
        self.lead = self.fields * self.each
        self.cols = PROWS * self.bw
        self.full = self.cols // LANES
        self.rest = self.cols % LANES
        self.share = LANES // self.rest
        self.octets = self.lead // 8
        self.rest_octets = -(-self.octets // self.share)
        self.packed = self.full * self.lead + 8 * self.rest_octets
        self.point_tiles = self.seg // LANES
        self.wide = -(-self.lead // LANES) * LANES

    def fold_scratch(self, tiles):
        rows = self.levels * tiles * self.forced
        return [
            pltpu.VMEM((self.fields, self.steps, self.levels, tiles, self.forced, LANES), jnp.float32),
            pltpu.VMEM((self.fields * NT * rows, LANES), jnp.float32),
            pltpu.SemaphoreType.DMA((self.fields,)),
        ]

    def point_scratch(self, zone):
        return [
            pltpu.VMEM((2, zone, self.seg), jnp.int32),
            pltpu.VMEM((2, zone, self.seg), jnp.float32),
            pltpu.SemaphoreType.DMA((4,)),
        ]


def fold_field(size, field, tiles, buffer, folded, steps_first=False):
    rows = size.levels * tiles * size.forced
    flat = buffer.reshape(*buffer.shape[:2], rows, LANES)

    def one_part(index, carry):
        part = pl.multiple_of(16 * index, 16)

        def write(k, value):
            start = (field * NT + k) * rows
            folded[pl.ds(start + part, 16), :] = value

        fold_times(
            lambda t: flat[t, field, pl.ds(part, 16)] if steps_first else flat[field, t, pl.ds(part, 16)],
            write,
            size.steps,
        )
        return carry

    lax.fori_loop(0, rows // 16, one_part, 0)


def folded_rows(size, folded, first_field, count, tiles, tile, row):
    rows = size.levels * tiles * size.forced
    start = first_field * NT * rows + tile * size.forced + row
    return folded[pl.ds(start, count * size.each, stride=tiles * size.forced), :]


def start_points(point_refs, ints, floats, sems):
    copies = []
    for index, ref in enumerate(point_refs):
        target = (ints if index < 2 else floats).at[index % 2]
        copy = pltpu.make_async_copy(ref, target, sems.at[index])
        copy.start()
        copies.append(copy)
    return copies


def block_stencil(size, me, block, first_tile, ints, floats, right_hi, right_lo):
    center, diffuse = zone_factors(size.forced)
    window = 2 * LANES
    lanes = pl.ds(pl.multiple_of(first_tile * LANES, LANES), window)
    zone = ints.shape[1]
    lane = lax.broadcasted_iota(jnp.int32, (zone, window), 1)
    third = divided_by_3(first_tile * LANES + lane)
    first_col = first_columns(ints[0, :, lanes], third, me * size.par, size.total) - block * size.bw
    col_weights = lagrange_weights(floats[0, :, lanes])
    row_weights = lagrange_weights(floats[1, :, lanes])
    first_row = ints[1, :, lanes]

    def shifted(value, shift):
        if shift == 0:
            return value
        return pltpu.roll(value, (-shift) % window, 1)

    column = lax.broadcasted_iota(jnp.int32, (size.bw, LANES), 0)
    prow = lax.broadcasted_iota(jnp.int32, (8, LANES), 0)
    source = {}
    for shift in (-1, 0, 1):
        base = shifted(first_col, shift)
        if shift == -1:
            base = jnp.where(lane == 0, FAR, base)
        if shift == 1:
            base = jnp.where(lane == window - 1, FAR, base)
        source[shift] = (
            base,
            [shifted(w, shift) for w in col_weights],
            shifted(first_row, shift),
            [shifted(w, shift) for w in row_weights],
        )
    for half in range(2):
        part = slice(half * LANES, (half + 1) * LANES)
        tables = {}
        for row in range(size.forced):
            for zone_row, shift, _ in diffused_terms(row, size.forced, center, diffuse):
                if (zone_row, shift) in tables:
                    continue
                base, col_w, base_row, row_w = source[shift]
                one = slice(zone_row, zone_row + 1)
                tables[zone_row, shift] = (
                    tap_select(column - base[one, part], [w[one, part] for w in col_w]),
                    tap_select(prow - base_row[one, part], [w[one, part] for w in row_w]),
                )
        for row in range(size.forced):
            terms = [
                (tables[zone_row, shift][0], tables[zone_row, shift][1] * factor)
                for zone_row, shift, factor in diffused_terms(row, size.forced, center, diffuse)
            ]
            depth = slice(row * window + half * LANES, row * window + (half + 1) * LANES)
            for pair in range(PROWS // 2):
                pieces = []
                for p in (2 * pair, 2 * pair + 1):
                    products = [col_w * row_w[p : p + 1] for col_w, row_w in terms]
                    pieces.append(functools.reduce(jnp.add, products))
                high, low = split_bf16(jnp.concatenate(pieces, axis=0))
                rows = slice(2 * pair * size.bw, 2 * (pair + 1) * size.bw)
                right_hi[rows, depth] = high
                right_lo[rows, depth] = low


def spill_hits(size, entry, column, at_left, at_right):
    side = (entry // SPILL_ROWS) & 1
    inner = entry & (SPILL_ROWS - 1)
    target = (inner >> 2) * size.bw + (inner & 3)
    on_left = (side == 0) & at_left & (column == target)
    on_right = (side == 1) & at_right & (column == target + size.bw - SPILL)
    return jnp.where((inner < PROWS * SPILL) & (on_left | on_right), 1.0, 0.0).astype(jnp.bfloat16)


def block_of(size, owner_ref, dest):
    block = jnp.int32(0)
    for candidate in range(size.tiles):
        block = block + jnp.where(owner_ref[0, candidate] == dest, candidate, 0)
    return block


def pack_rest(size, rest, out_ref):
    rest = jnp.concatenate([rest, jnp.zeros((size.lead, LANES - size.rest), jnp.float32)], axis=1)
    for octet in range(size.rest_octets):
        packed = None
        for member in range(size.share):
            index = member * size.rest_octets + octet
            if index >= size.octets:
                continue
            piece = rest[8 * index : 8 * index + 8]
            if member:
                piece = pltpu.roll(piece, member * size.rest, 1)
            packed = piece if packed is None else packed + piece
        start = size.full * size.lead + 8 * octet
        out_ref[start : start + 8] = packed


def product(left, right_hi, right_lo):
    contract = (((1,), (1,)), ((), ()))
    count = left.shape[0] // 2
    both = lax.dot_general(left, right_hi, contract, preferred_element_type=jnp.float32)
    extra = lax.dot_general(left[:count], right_lo, contract, preferred_element_type=jnp.float32)
    return both[:count] + both[count:] + extra


def window_of(size, block):
    first = jnp.maximum(3 * size.bw * block - 10, 0) // LANES
    return jnp.minimum(first, size.point_tiles - 2)


def first_call(size, step, owner, cotangent, points):
    zone = points[0].shape[0]
    window = 2 * LANES
    depth = size.forced * window
    chunks = ((0, size.fields - 2), (size.fields - 2, size.fields))

    def kernel(owner_hbm, cot_ref, *refs):
        point_refs, out_ref, edge_refs, refs = refs[:4], refs[4], refs[5:7], refs[7:]
        owner_ref, owner_sem, buffer, folded, sems, ints, floats, point_sems, left, right_hi, right_lo = refs[:-3]
        edge_buffer, edge_folded, edge_sems = refs[-3:]
        owner_copy = pltpu.make_async_copy(owner_hbm, owner_ref, owner_sem)
        owner_copy.start()
        point_copies = start_points(point_refs, ints, floats, point_sems)
        edge_copies = []
        for end, tile in enumerate((0, size.point_tiles - 1)):
            copy = pltpu.make_async_copy(
                cot_ref.at[:, :, :, pl.ds(tile, 1)], edge_buffer.at[:, :, :, pl.ds(end, 1)], edge_sems.at[end]
            )
            copy.start()
            edge_copies.append(copy)
        me = lax.axis_index("tile")
        owner_copy.wait()
        block = block_of(size, owner_ref, me ^ step)
        first_tile = window_of(size, block)
        copies = []
        for field in range(size.fields):
            copy = pltpu.make_async_copy(
                cot_ref.at[:, field, :, pl.ds(first_tile, 2)], buffer.at[field], sems.at[field]
            )
            copy.start()
            copies.append(copy)
        for copy in point_copies:
            copy.wait()
        center, diffuse = zone_factors(size.forced)
        lane = lax.broadcasted_iota(jnp.int32, (zone, LANES), 1)
        entry = lax.broadcasted_iota(jnp.int32, (SPILL_ROWS, LANES), 0)
        entry_lane = lax.broadcasted_iota(jnp.int32, (SPILL_ROWS, LANES), 1)
        parent_row = entry >> 2
        stencils = []
        for tile, edge_lane, out_start in ((0, 0, -SPILL), (size.point_tiles - 1, LANES - 1, size.par)):
            part = slice(tile * LANES, (tile + 1) * LANES)
            third = divided_by_3(tile * LANES + lane)
            first_col = first_columns(ints[0, :, part], third, me * size.par, size.total)
            own = [first_col, ints[1, :, part]]
            own += lagrange_weights(floats[0, :, part]) + lagrange_weights(floats[1, :, part])
            source = {0: own}
            for shift in (-1, 1):
                moved = [pltpu.roll(value, (-shift) % LANES, 1) for value in own]
                moved[0] = jnp.where(lane == (0 if shift == -1 else LANES - 1), FAR, moved[0])
                source[shift] = moved

            def one(values, row):
                rows = [value[row : row + 1] for value in values]
                along = tap_select((entry & 3) + out_start - rows[0], rows[2:6])
                across = tap_select(parent_row - rows[1], rows[6:10])
                return along * across

            stencil = []
            for row in range(size.forced):
                terms = [
                    one(source[shift], zone_row) * factor
                    for zone_row, shift, factor in diffused_terms(row, size.forced, center, diffuse)
                ]
                picks = (entry == PROWS * SPILL + row - 1) & (entry_lane == edge_lane) & (row > 0)
                stencil.append(jnp.where(picks, 1.0, functools.reduce(jnp.add, terms)))
            stencils.append(jnp.concatenate(stencil, axis=1))

        for copy in edge_copies:
            copy.wait()
        for field in range(size.fields):
            fold_field(size, field, 2, edge_buffer, edge_folded, steps_first=True)
        contract = (((1,), (1,)), ((), ()))
        for end in range(2):
            parts = []
            for row in range(size.forced):
                values = folded_rows(size, edge_folded, 0, size.fields, 2, end, row)
                parts.append(jnp.concatenate(split_bf16(values), axis=0))
            right = jnp.concatenate(parts, axis=1)
            high, low = split_bf16(stencils[end])
            both = lax.dot_general(high, right, contract, preferred_element_type=jnp.float32)
            extra = lax.dot_general(low, right[: size.lead], contract, preferred_element_type=jnp.float32)
            edge_ref = edge_refs[end]
            edge_ref[...] = jnp.zeros((EDGE_ROWS, size.wide), jnp.float32)
            edge_ref[:SPILL_ROWS, : size.lead] = both[:, : size.lead] + both[:, size.lead :] + extra
            point = 0 if end == 0 else size.seg - 1
            start = PROWS * SPILL + size.forced - 1
            for kind in range(4):
                for row in range(1, size.forced):
                    value = (ints if kind < 2 else floats)[kind % 2, row : row + 1, point : point + 1]
                    edge_ref[start : start + 1] = jnp.broadcast_to(value.astype(jnp.float32), (1, size.wide))
                    start += 1
        block_stencil(size, me, block, first_tile, ints, floats, right_hi, right_lo)
        pieces = []
        for first, last in chunks:
            for field in range(first, last):
                copies[field].wait()
                fold_field(size, field, 2, buffer, folded)
            base, count = 2 * first * size.each, (last - first) * size.each
            for half in range(2):
                for row in range(size.forced):
                    high, low = split_bf16(folded_rows(size, folded, first, last - first, 2, half, row))
                    part = slice(row * window + half * LANES, row * window + (half + 1) * LANES)
                    left[base : base + count, part] = high
                    left[base + count : base + 2 * count, part] = low
            result = product(left[base : base + 2 * count], right_hi[...], right_lo[...])
            for tile in range(size.full):
                start = tile * size.lead + first * size.each
                out_ref[start : start + count] = result[:, tile * LANES : (tile + 1) * LANES]
            pieces.append(result[:, size.full * LANES :])
        pack_rest(size, jnp.concatenate(pieces, axis=0), out_ref)

    vmem = pl.BlockSpec(memory_space=pltpu.VMEM)
    hbm = pl.BlockSpec(memory_space=pltpu.HBM)
    return pl.pallas_call(
        kernel,
        out_shape=[pltpu.VMEM((size.packed, LANES), jnp.float32)]
        + [pltpu.VMEM((EDGE_ROWS, size.wide), jnp.float32)] * 2,
        in_specs=[hbm] * 6,
        out_specs=[vmem] * 3,
        scratch_shapes=[pltpu.SMEM((1, size.tiles), jnp.int32), pltpu.SemaphoreType.DMA]
        + size.fold_scratch(2)
        + size.point_scratch(zone)
        + [
            pltpu.VMEM((2 * size.lead, depth), jnp.bfloat16),
            pltpu.VMEM((size.cols, depth), jnp.bfloat16),
            pltpu.VMEM((size.cols, depth), jnp.bfloat16),
            pltpu.VMEM((size.steps, size.fields, size.levels, 2, size.forced, LANES), jnp.float32),
            pltpu.VMEM((size.lead * 2 * size.forced, LANES), jnp.float32),
            pltpu.SemaphoreType.DMA((2,)),
        ],
        compiler_params=pltpu.CompilerParams(vmem_limit_bytes=VMEM_BYTES),
        name=f"block_{step}",
    )(in_hbm(owner), in_hbm(cotangent), *map(in_hbm, points))


def write_blocks(size, steps, owner_ref, parts_ref, ints, floats, across_ref, out_refs, right_hi, right_lo):
    inner = size.forced * 2 * LANES
    me = lax.axis_index("tile")
    for step, out_ref in zip(steps, out_refs):
        block = block_of(size, owner_ref, me ^ step)
        first_tile = window_of(size, block)
        block_stencil(size, me, block, first_tile, ints, floats, right_hi, right_lo)
        left = [
            parts_ref[first_tile + half, row] for row in range(size.forced) for half in range(2)
        ]
        left.append(across_ref[...])
        column = lax.broadcasted_iota(jnp.int32, (size.cols, LANES), 0)
        entry = lax.broadcasted_iota(jnp.int32, (size.cols, LANES), 1)
        right_hi[:, inner:] = spill_hits(size, entry, column, block == 0, block == size.tiles - 1)
        right_lo[:, inner:] = jnp.zeros((size.cols, LANES), jnp.bfloat16)
        result = product(jnp.concatenate(left, axis=1), right_hi[...], right_lo[...])
        for tile in range(size.full):
            start = tile * size.lead
            out_ref[start : start + size.lead] = result[:, tile * LANES : (tile + 1) * LANES]
        pack_rest(size, result[:, size.full * LANES :], out_ref)


def block_call(size, steps, owner, parts, ints, floats, across, fix=None, after=(), unread=()):
    depth = size.forced * 2 * LANES + LANES

    def kernel(owner_ref, parts_ref, ints, floats, across_ref, *refs):
        if fix is not None:
            fix_ref, refs = refs[0], refs[1:]
        refs = refs[len(after) + len(unread) :]
        out_refs, refs = refs[: len(steps)], refs[len(steps) :]
        if fix is not None:
            refs[0][...] = fix_ref[...]
            refs = refs[1:]
        right_hi, right_lo = refs
        write_blocks(size, steps, owner_ref, parts_ref, ints, floats, across_ref, out_refs, right_hi, right_lo)

    vmem = pl.BlockSpec(memory_space=pltpu.VMEM)
    operands = [parts, ints, floats, across] + ([] if fix is None else [fix]) + list(after)
    outs = [pltpu.VMEM((size.packed, LANES), jnp.float32)] * len(steps)
    if fix is not None:
        outs.append(pltpu.VMEM((SPILL_ROWS, size.wide), jnp.float32))
    return pl.pallas_call(
        kernel,
        out_shape=outs,
        in_specs=[pl.BlockSpec(memory_space=pltpu.SMEM)]
        + [vmem] * len(operands)
        + [pl.BlockSpec(memory_space=pltpu.HBM)] * len(unread),
        out_specs=[vmem] * len(outs),
        scratch_shapes=[pltpu.VMEM((size.cols, depth), jnp.bfloat16)] * 2,
        compiler_params=pltpu.CompilerParams(vmem_limit_bytes=BLOCK_VMEM),
        name="block_" + "_".join(map(str, steps)),
    )(owner, *map(in_vmem, operands), *map(in_hbm, unread))


def in_vmem(array):
    return pltpu.with_memory_space_constraint(array, pltpu.VMEM)


def in_hbm(array):
    return pltpu.with_memory_space_constraint(array, pltpu.HBM)


def fold_call(size, cotangent, points, after):
    zone = points[0].shape[0]

    def kernel(cot_ref, *refs):
        point_refs, parts_ref, ints, floats, buffer, folded, sems, point_sems = refs[:4], *refs[4 + len(after) :]
        point_copies = start_points(point_refs, ints, floats, point_sems)
        copies = []
        for field in range(size.fields):
            copy = pltpu.make_async_copy(cot_ref.at[:, field], buffer.at[field], sems.at[field])
            copy.start()
            copies.append(copy)
        for copy in point_copies:
            copy.wait()
        for field in range(size.fields):
            copies[field].wait()
            fold_field(size, field, size.point_tiles, buffer, folded)
            rows = slice(field * size.each, (field + 1) * size.each)
            low_rows = slice(size.lead + field * size.each, size.lead + (field + 1) * size.each)
            for tile in range(size.point_tiles):
                for row in range(size.forced):
                    values = folded_rows(size, folded, field, 1, size.point_tiles, tile, row)
                    parts_ref[tile, row, rows], parts_ref[tile, row, low_rows] = split_bf16(values)

    vmem = pl.BlockSpec(memory_space=pltpu.VMEM)
    hbm = pl.BlockSpec(memory_space=pltpu.HBM)
    return pl.pallas_call(
        kernel,
        out_shape=[
            pltpu.VMEM((size.point_tiles, size.forced, 2 * size.lead, LANES), jnp.bfloat16),
            pltpu.VMEM((2, zone, size.seg), jnp.int32),
            pltpu.VMEM((2, zone, size.seg), jnp.float32),
        ],
        in_specs=[hbm] * 5 + [vmem] * len(after),
        out_specs=[vmem] * 3,
        scratch_shapes=size.fold_scratch(size.point_tiles) + size.point_scratch(zone)[2:],
        compiler_params=pltpu.CompilerParams(vmem_limit_bytes=VMEM_BYTES),
        name="fold",
    )(in_hbm(cotangent), *map(in_hbm, points), *map(in_vmem, after))


def join_call(size, early, step, owner, edges, from_left, from_right, parts, ints, floats):
    depth = size.forced * 2 * LANES + LANES

    def kernel(owner_ref, *refs):
        left_ref, right_ref, from_left_ref, from_right_ref, parts_ref, ints, floats = refs[:7]
        across_ref, fix_ref, out_ref, right_hi, right_lo = refs[7:]
        me = lax.axis_index("tile")
        _, diffuse = zone_factors(size.forced)
        entry = lax.broadcasted_iota(jnp.int32, (SPILL_ROWS, size.wide), 0)
        spills = []
        for own_ref, other_ref, own_point, other_third, first in (
            (left_ref, from_left_ref, 0, -1, 0),
            (right_ref, from_right_ref, size.seg - 1, size.par, size.par - SPILL),
        ):
            total = other_ref[:SPILL_ROWS]
            column = (entry & 3) + first
            for row in range(1, size.forced):
                start = PROWS * SPILL + size.forced - 1

                def stencil(ref, third):
                    kinds = [
                        ref[start + kind * (size.forced - 1) + row - 1 :][:1] for kind in range(4)
                    ]
                    cols = kinds[0].astype(jnp.int32)
                    base = first_columns(cols, jnp.full_like(cols, third), me * size.par, size.total)
                    along = tap_select(column - base, lagrange_weights(kinds[2]))
                    across = tap_select((entry >> 2) - kinds[1].astype(jnp.int32), lagrange_weights(kinds[3]))
                    return along * across

                folded_row = PROWS * SPILL + row - 1
                here = stencil(own_ref, own_point // 3) * other_ref[folded_row : folded_row + 1]
                there = stencil(other_ref, other_third) * own_ref[folded_row : folded_row + 1]
                total = total - diffuse[row] * (here + there)
            spills.append(jnp.where(entry < PROWS * SPILL, total, 0.0))
        blank = jnp.zeros((LANES - 2 * SPILL_ROWS, size.wide), jnp.float32)
        across = jnp.transpose(jnp.concatenate(spills + [blank], axis=0))[: size.lead]
        across_ref[: size.lead], across_ref[size.lead :] = split_bf16(across)
        fixed = block_of(size, owner_ref, me ^ early)
        fix = jnp.where(fixed == 0, spills[0], jnp.where(fixed == size.tiles - 1, spills[1], 0.0))
        flag = jnp.where(fixed == 0, 1.0, 0.0)
        fix_ref[...] = jnp.where(entry == SPILL_ROWS - 1, flag, fix)
        write_blocks(
            size, [step], owner_ref, parts_ref, ints, floats, across_ref, [out_ref], right_hi, right_lo
        )

    vmem = pl.BlockSpec(memory_space=pltpu.VMEM)
    return pl.pallas_call(
        kernel,
        out_shape=[
            pltpu.VMEM((2 * size.lead, LANES), jnp.bfloat16),
            pltpu.VMEM((SPILL_ROWS, size.wide), jnp.float32),
            pltpu.VMEM((size.packed, LANES), jnp.float32),
        ],
        in_specs=[pl.BlockSpec(memory_space=pltpu.SMEM)] + [vmem] * 7,
        out_specs=[vmem] * 3,
        scratch_shapes=[pltpu.VMEM((size.cols, depth), jnp.bfloat16)] * 2,
        compiler_params=pltpu.CompilerParams(vmem_limit_bytes=BLOCK_VMEM),
        name="join",
    )(owner, *map(in_vmem, [*edges, from_left, from_right, parts, ints, floats]))


def fix_call(size, block, fix):
    def kernel(block_ref, fix_ref, out_ref):
        values = fix_ref[...]
        values = jnp.concatenate(
            [values, jnp.zeros((LANES - SPILL_ROWS, size.wide), jnp.float32)], axis=0
        )
        across = jnp.transpose(values)[: size.lead]
        at_left = fix_ref[SPILL_ROWS - 1, 0] > 0.5
        column = lax.broadcasted_iota(jnp.int32, (size.cols, LANES), 0)
        entry = lax.broadcasted_iota(jnp.int32, (size.cols, LANES), 1)
        hits = [
            spill_hits(size, entry + SPILL_ROWS * side, column, side == 0, side == 1) for side in range(2)
        ]
        inside = entry < SPILL_ROWS
        right = jnp.where(at_left, hits[0].astype(jnp.float32), hits[1].astype(jnp.float32))
        right = jnp.where(inside, right, 0.0).astype(jnp.bfloat16)
        high, low = split_bf16(across)
        contract = (((1,), (1,)), ((), ()))
        both = lax.dot_general(
            jnp.concatenate([high, low], axis=0), right, contract, preferred_element_type=jnp.float32
        )
        result = both[: size.lead] + both[size.lead :]
        for tile in range(size.full):
            rows = slice(tile * size.lead, (tile + 1) * size.lead)
            out_ref[rows] = block_ref[rows] + result[:, tile * LANES : (tile + 1) * LANES]
        rows = slice(size.full * size.lead, size.packed)
        pack_rest(size, result[:, size.full * LANES :], out_ref)
        out_ref[rows] += block_ref[rows]

    vmem = pl.BlockSpec(memory_space=pltpu.VMEM)
    return pl.pallas_call(
        kernel,
        out_shape=pltpu.VMEM((size.packed, LANES), jnp.float32),
        in_specs=[vmem] * 2,
        out_specs=vmem,
        compiler_params=pltpu.CompilerParams(vmem_limit_bytes=VMEM_BYTES),
        name="fix",
    )(in_vmem(block), in_vmem(fix))


def pieces(size, source, member):
    for p in range(PROWS):
        done = 0
        while done < size.bw:
            from_lane = p * size.bw + done
            to_lane = source * size.bw + done
            count = min(size.bw - done, LANES - from_lane % LANES, LANES - to_lane % LANES)
            held = from_lane // LANES
            extra = member * size.rest if held == size.full else 0
            start = to_lane % LANES
            yield p, to_lane // LANES, start, start + count, held, (to_lane - from_lane - extra) % LANES
            done += count


def each_octet(size, one_octet):
    def body(i, carry):
        for member in range(size.share):
            octet = member * size.rest_octets + i
            if (member + 1) * size.rest_octets <= size.octets:
                one_octet(octet, member)
            else:
                pl.when(octet < size.octets)(functools.partial(one_octet, octet, member))
        return carry

    lax.fori_loop(0, size.rest_octets, body, 0)


def octet_rows(size, octet, member):
    rows = [pl.ds(pl.multiple_of(tile * size.lead + 8 * octet, 8), 8) for tile in range(size.full)]
    start = size.full * size.lead + 8 * (octet - member * size.rest_octets)
    return rows + [pl.ds(pl.multiple_of(start, 8), 8)]


def octet_pairs(size, octet):
    per_octet = 8 // size.levels
    field = octet // (NT // per_octet)
    time = per_octet * (octet - field * (NT // per_octet))
    return [(time + k) * size.fields + field for k in range(per_octet)]


def merge(size, refs, position, octet, member, merged):
    lane = lax.broadcasted_iota(jnp.int32, (8, LANES), 1)
    rows = octet_rows(size, octet, member)
    for source in range(size.tiles):
        if source ^ position not in refs:
            continue
        tiles = [refs[source ^ position][r] for r in rows]
        for p, tile, start, stop, held, shift in pieces(size, source, member):
            value = pltpu.roll(tiles[held], shift, 1) if shift else tiles[held]
            if (p, tile) in merged:
                value = jnp.where((lane >= start) & (lane < stop), value, merged[p, tile])
            merged[p, tile] = value


def at_position(size, one_octet):
    me = lax.axis_index("tile")
    for position in range(size.tiles):
        pl.when(me == position)(functools.partial(each_octet, size, functools.partial(one_octet, position)))


def place_call(size, arrived, unread):
    shape = (size.octets, PROWS, size.par // LANES, 8, LANES)

    def kernel(*refs):
        blocks, staged = dict(zip(arrived, refs)), refs[-1]

        def one_octet(position, octet, member):
            merged = {}
            merge(size, blocks, position, octet, member, merged)
            for (p, tile), value in merged.items():
                staged[octet, p, tile] = value

        at_position(size, one_octet)

    vmem = pl.BlockSpec(memory_space=pltpu.VMEM)
    return pl.pallas_call(
        kernel,
        out_shape=pltpu.VMEM(shape, jnp.float32),
        in_specs=[vmem] * len(arrived) + [pl.BlockSpec(memory_space=pltpu.HBM)],
        out_specs=vmem,
        compiler_params=pltpu.CompilerParams(vmem_limit_bytes=BLOCK_VMEM),
        name="place",
    )(*map(in_vmem, arrived.values()), in_hbm(unread))


def finish_call(size, staged, arrived):
    shape = (NT * size.fields, PROWS, size.levels, size.par)

    def kernel(staged_ref, *refs):
        blocks, (out_ref, final, sem) = dict(zip(arrived, refs)), refs[len(arrived) :]

        def one_octet(position, octet, member):
            merged = {
                (p, tile): staged_ref[octet, p, tile]
                for p in range(PROWS)
                for tile in range(size.par // LANES)
            }
            merge(size, blocks, position, octet, member, merged)
            for k, pair in enumerate(octet_pairs(size, octet)):
                for (p, tile), value in merged.items():
                    part = slice(tile * LANES, (tile + 1) * LANES)
                    final[pair, p, :, part] = value[k * size.levels : (k + 1) * size.levels]
                pltpu.make_async_copy(final.at[pair], out_ref.at[pair], sem).start()

        at_position(size, one_octet)
        pltpu.make_async_copy(final, out_ref, sem).wait()

    vmem = pl.BlockSpec(memory_space=pltpu.VMEM)
    return pl.pallas_call(
        kernel,
        out_shape=jax.ShapeDtypeStruct(shape, jnp.float32),
        in_specs=[vmem] * (1 + len(arrived)),
        out_specs=pl.BlockSpec(memory_space=pltpu.HBM),
        scratch_shapes=[pltpu.VMEM(shape, jnp.float32), pltpu.SemaphoreType.DMA],
        compiler_params=pltpu.CompilerParams(vmem_limit_bytes=BLOCK_VMEM),
        name="finish",
    )(in_vmem(staged), *map(in_vmem, arrived.values()))


def more_call(size, staged, arrived, unread):
    shape = staged.shape

    def kernel(*refs):
        blocks, staged_ref = dict(zip(arrived, refs[1:])), refs[-1]

        def one_octet(position, octet, member):
            touched = {
                source ^ position: [
                    (p, tile) for p, tile, *_ in pieces(size, source, member)
                ]
                for source in range(size.tiles)
                if source ^ position in blocks
            }
            merged = {
                (p, tile): staged_ref[octet, p, tile] for keys in touched.values() for p, tile in keys
            }
            merge(size, blocks, position, octet, member, merged)
            for (p, tile), value in merged.items():
                staged_ref[octet, p, tile] = value

        at_position(size, one_octet)

    vmem = pl.BlockSpec(memory_space=pltpu.VMEM)
    return pl.pallas_call(
        kernel,
        out_shape=pltpu.VMEM(shape, jnp.float32),
        in_specs=[vmem] * (1 + len(arrived)) + [pl.BlockSpec(memory_space=pltpu.HBM)],
        out_specs=vmem,
        input_output_aliases={0: 0},
        compiler_params=pltpu.CompilerParams(vmem_limit_bytes=BLOCK_VMEM),
        name="more",
    )(in_vmem(staged), *map(in_vmem, arrived.values()), in_hbm(unread))


def shards(cotangent, stencil_col, stencil_row, frac_along, frac_across, owner_map):
    tiles = lax.axis_size("tile")
    size = Sizes(cotangent.shape, tiles)
    points = (stencil_col, stencil_row, frac_along, frac_across)
    up = [(i, (i + 1) % tiles) for i in range(tiles)]
    down = [(j, i) for i, j in up]
    tiled = cotangent.reshape(cotangent.shape[:-1] + (size.point_tiles, LANES))
    tiled = jnp.transpose(tiled, (0, 1, 2, 4, 3, 5))
    half = tiles // 2
    far, near = list(range(half, tiles)), list(range(half - 1, 0, -1))
    arrived = [None] * tiles

    def send(step, value):
        return lax.ppermute(value, "tile", [(i, i ^ step) for i in range(tiles)])

    early = far[0]
    first, *edges = first_call(size, early, owner_map, tiled, points)
    arrived[early] = send(early, first)
    from_right = lax.ppermute(edges[0], "tile", down)
    from_left = lax.ppermute(edges[1], "tile", up)
    parts, ints, floats = fold_call(size, tiled, points, edges)
    across, fix, block = join_call(
        size, early, far[1], owner_map, edges, from_left, from_right, parts, ints, floats
    )
    arrived[far[1]] = send(far[1], block)
    made = [block]
    turns = [kind[i : i + 2] for kind in (far[2:], near) for i in range(0, len(kind), 2)]
    for turn in turns:
        fixes = turn[0] == near[0]
        after = list(made[:1]) + ([arrived[early]] if fixes else [])
        made = block_call(size, turn, owner_map, parts, ints, floats, across, fix if fixes else None, after)
        for step, block in zip(turn, made):
            arrived[step] = send(step, block)
        if fixes:
            fix = send(early, made[-1])
    arrived[0] = block_call(size, [0], owner_map, parts, ints, floats, across)[0]
    arrived[early] = fix_call(size, arrived[early], fix)
    staged = place_call(size, {step: arrived[step] for step in (far[1], early, 0)}, tiled)
    for turn in turns[:-1]:
        staged = more_call(size, staged, {step: arrived[step] for step in turn}, tiled)
    placed = finish_call(size, staged, {step: arrived[step] for step in turns[-1]})
    placed = placed.reshape(NT, size.fields, PROWS, size.levels, size.par)
    return jnp.transpose(placed, (0, 1, 3, 2, 4))


def solution(mesh):
    in_specs = (
        P(None, None, "lev", None, ("ens", "tile")),
        P(None, ("ens", "tile")),
        P(None, ("ens", "tile")),
        P(None, ("ens", "tile")),
        P(None, ("ens", "tile")),
        P(("ens", "tile"), None),
    )
    out_specs = P(None, None, "lev", None, ("ens", "tile"))
    return jax.shard_map(shards, mesh=mesh, in_specs=in_specs, out_specs=out_specs, check_vma=False)
```

profile of v0, /device:TPU:0, one launch (start us, length us, event | category | flops | bytes accessed | tf_op | source)
XLA Modules:
  0.0 68.3 jit_solution(192112077928962465)
XLA Ops:
  0.0 5.4 %block_4.1 = (f32[544,128]{1,0:T(8,128)S(1)}, f32[40,256]{1,0:T(8,128)S(1)}, f32[40,256]{1,0:T(8,128)S(1)}) custom-call(s32[1,8]{1,0:T(1,128)} %owner_ref.9, f32[34,5,4,9,4,128]{5,4,3,2,1,0:T(4,128)} %bitcast.6, s32[5,1152]{1,0:T(8,128)} %refs_0_.3, s32[5,1152]{1,0:T(8,128)} %refs_1_.3, f32[5,1152]{1,0:T(8,128)} %refs_2_.3, f32[5,1152]{1,0:T(8,128)} %refs_3_.3), custom_call_target="tpu_custom_call" | custom-call | tf_op jit(solution)/shard_map/block_4/pallas_call | solution.py:380
  5.4 3.0 %collective-permute-start = (f32[40,256]{1,0:T(8,128)S(1)}, f32[40,256]{1,0:T(8,128)S(1)}, u32[]{:S(2)}, u32[]{:S(2)}) collective-permute-start(f32[40,256]{1,0:T(8,128)S(1)} %get-tuple-element.20.refs_5_.refs_1_), channel_id=1, source_target_pairs={{0,2},{2,4},{4,6},{6,8},{8,10},{10,12},{12,14},{14,0},{1,3},{3,5},... | collective-permute-start | bytes 122888 | tf_op jit(solution)/shard_map/ppermute | solution.py:778
  8.4 3.1 %collective-permute-start.1 = (f32[40,256]{1,0:T(8,128)S(1)}, f32[40,256]{1,0:T(8,128)S(1)}, u32[]{:S(2)}, u32[]{:S(2)}) collective-permute-start(f32[40,256]{1,0:T(8,128)S(1)} %get-tuple-element.19.refs_4_.refs_0_), channel_id=1, source_target_pairs={{2,0},{4,2},{6,4},{8,6},{10,8},{12,10},{14,12},{0,14},{3,1},{5,3},... | collective-permute-start | bytes 122888 | tf_op jit(solution)/shard_map/ppermute | solution.py:777
  11.5 0.9 %collective-permute-start.3 = (f32[544,128]{1,0:T(8,128)S(1)}, f32[544,128]{1,0:T(8,128)S(1)}, u32[]{:S(2)}, u32[]{:S(2)}) collective-permute-start(f32[544,128]{1,0:T(8,128)S(1)} %get-tuple-element.25), channel_id=1, source_target_pairs={{0,8},{2,10},{4,12},{6,14},{8,0},{10,2},{12,4},{14,6},{1,9},{3,11}... | collective-permute-start | bytes 835592 | tf_op jit(solution)/shard_map/ppermute | solution.py:772
  12.4 5.6 %fold.1 = (bf16[9,4,480,128]{3,2,1,0:T(8,128)(2,1)S(1)}, s32[2,5,1152]{2,1,0:T(8,128)S(1)}, f32[2,5,1152]{2,1,0:T(8,128)S(1)}) custom-call(f32[34,5,4,9,4,128]{5,4,3,2,1,0:T(4,128)} %bitcast.7, s32[5,1152]{1,0:T(8,128)} %refs_0_.3, s32[5,1152]{1,0:T(8,128)} %refs_1_.3, f32[5,1152]{1,0:T(8,128)} %refs_2_.3, f32[5,1152]{1,0:T(8,128)} %refs_3_.3, ...), custom_call_target="tpu_custom_call" | custom-call | tf_op jit(solution)/shard_map/fold/pallas_call | solution.py:489
  18.0 0.0 collective-permute-done.refs_2_
  18.0 0.0 collective-permute-done.1.refs_3_
  18.0 2.7 %join.1 = (bf16[480,128]{1,0:T(8,128)(2,1)S(1)}, f32[32,256]{1,0:T(8,128)S(1)}, f32[544,128]{1,0:T(8,128)S(1)}) custom-call(s32[1,8]{1,0:T(1,128)S(1)} %copy-done, f32[40,256]{1,0:T(8,128)S(1)} %get-tuple-element.19.refs_4_.refs_0_, f32[40,256]{1,0:T(8,128)S(1)} %get-tuple-element.20.refs_5_.refs_1_, f32[40,256]{1,0:T(8,128)S(1)} %collective-permute-done.refs_2_, ...), custom_call_target="tpu_custom_call" | custom-call | tf_op jit(solution)/shard_map/join/pallas_call | solution.py:550
  20.7 0.5 collective-permute-start.2
  21.2 3.9 %block_6_7.1 = (f32[544,128]{1,0:T(8,128)S(1)}, f32[544,128]{1,0:T(8,128)S(1)}) custom-call(s32[1,8]{1,0:T(1,128)S(1)} %copy-done, bf16[9,4,480,128]{3,2,1,0:T(8,128)(2,1)S(1)} %get-tuple-element.21.refs_4_.parts_ref, s32[2,5,1152]{2,1,0:T(8,128)S(1)} %get-tuple-element.22.refs_5_.ints, f32[2,5,1152]{2,1,0:T(8,128)S(1)} %get-tuple-element.23.refs_6_.floats, ...), custom_call_target="tpu_custom_call" | custom-call | tf_op jit(solution)/shard_map/block_6_7/pallas_call | solution.py:443
  25.1 7.5 %collective-permute-done.3.refs_2_.block_ref = f32[544,128]{1,0:T(8,128)S(1)} collective-permute-done((f32[544,128]{1,0:T(8,128)S(1)}, f32[544,128]{1,0:T(8,128)S(1)}, u32[]{:S(2)}, u32[]{:S(2)}) %collective-permute-start.3) | collective-permute-done | bytes 278560 | tf_op jit(solution)/shard_map/ppermute | solution.py:772
  32.6 3.9 %block_3_2.1 = (f32[544,128]{1,0:T(8,128)S(1)}, f32[544,128]{1,0:T(8,128)S(1)}, f32[32,256]{1,0:T(8,128)S(1)}) custom-call(s32[1,8]{1,0:T(1,128)S(1)} %copy-done, bf16[9,4,480,128]{3,2,1,0:T(8,128)(2,1)S(1)} %get-tuple-element.21.refs_4_.parts_ref, s32[2,5,1152]{2,1,0:T(8,128)S(1)} %get-tuple-element.22.refs_5_.ints, ...), custom_call_target="tpu_custom_call" | custom-call | tf_op jit(solution)/shard_map/block_3_2/pallas_call | solution.py:443
  36.5 0.1 collective-permute-start.4
  36.5 2.1 %collective-permute-start.5 = (f32[544,128]{1,0:T(8,128)S(1)}, f32[544,128]{1,0:T(8,128)S(1)}, u32[]{:S(2)}, u32[]{:S(2)}) collective-permute-start(f32[544,128]{1,0:T(8,128)S(1)} %get-tuple-element.28.refs_1_), channel_id=1, source_target_pairs={{0,12},{2,14},{4,8},{6,10},{8,4},{10,6},{12,0},{14,2},{1,13},{3,15... | collective-permute-start | bytes 835592 | tf_op jit(solution)/shard_map/ppermute | solution.py:772
  38.6 0.8 %collective-permute-start.6 = (f32[544,128]{1,0:T(8,128)S(1)}, f32[544,128]{1,0:T(8,128)S(1)}, u32[]{:S(2)}, u32[]{:S(2)}) collective-permute-start(f32[544,128]{1,0:T(8,128)S(1)} %get-tuple-element.30), channel_id=1, source_target_pairs={{0,14},{2,12},{4,10},{6,8},{8,6},{10,4},{12,2},{14,0},{1,15},{3,13... | collective-permute-start | bytes 835592 | tf_op jit(solution)/shard_map/ppermute | solution.py:772
  39.5 2.3 %block_1.1 = f32[544,128]{1,0:T(8,128)S(1)} custom-call(s32[1,8]{1,0:T(1,128)S(1)} %copy-done, bf16[9,4,480,128]{3,2,1,0:T(8,128)(2,1)S(1)} %get-tuple-element.21.refs_4_.parts_ref, s32[2,5,1152]{2,1,0:T(8,128)S(1)} %get-tuple-element.22.refs_5_.ints, f32[2,5,1152]{2,1,0:T(8,128)S(1)} %get-tuple-element.23.refs_6_.floats, ...), custom_call_target="tpu_custom_call" | custom-call | tf_op jit(solution)/shard_map/block_1/pallas_call | solution.py:443
  41.8 2.6 %collective-permute-start.7 = (f32[544,128]{1,0:T(8,128)S(1)}, f32[544,128]{1,0:T(8,128)S(1)}, u32[]{:S(2)}, u32[]{:S(2)}) collective-permute-start(f32[544,128]{1,0:T(8,128)S(1)} %get-tuple-element.31.refs_0_), channel_id=1, source_target_pairs={{0,6},{2,4},{4,2},{6,0},{8,14},{10,12},{12,10},{14,8},{1,7},{3,5},... | collective-permute-start | bytes 835592 | tf_op jit(solution)/shard_map/ppermute | solution.py:772
  44.4 8.0 %collective-permute-done.4.fix_ref = f32[32,256]{1,0:T(8,128)S(1)} collective-permute-done((f32[32,256]{1,0:T(8,128)S(1)}, f32[32,256]{1,0:T(8,128)S(1)}, u32[]{:S(2)}, u32[]{:S(2)}) %collective-permute-start.4) | collective-permute-done | bytes 32800 | tf_op jit(solution)/shard_map/ppermute | solution.py:772
  52.4 0.0 collective-permute-start.8
  52.4 0.0 collective-permute-done.2.refs_0_
  52.4 0.0 collective-permute-start.9
  52.4 2.3 %block_0.1.refs_2_ = f32[544,128]{1,0:T(8,128)S(1)} custom-call(s32[1,8]{1,0:T(1,128)S(1)} %copy-done, bf16[9,4,480,128]{3,2,1,0:T(8,128)(2,1)S(1)} %get-tuple-element.21.refs_4_.parts_ref, s32[2,5,1152]{2,1,0:T(8,128)S(1)} %get-tuple-element.22.refs_5_.ints, f32[2,5,1152]{2,1,0:T(8,128)S(1)} %get-tuple-element.23.refs_6_.floats, ...), custom_call_target="tpu_custom_call" | custom-call | tf_op jit(solution)/shard_map/block_0/pallas_call | solution.py:443
  54.8 0.4 fix.1.refs_1_
  55.2 1.8 %place.1.refs_0_ = f32[30,6,3,8,128]{4,3,2,1,0:T(8,128)S(1)} custom-call(f32[544,128]{1,0:T(8,128)S(1)} %collective-permute-done.2.refs_0_, f32[544,128]{1,0:T(8,128)S(1)} %fix.1.refs_1_, f32[544,128]{1,0:T(8,128)S(1)} %block_0.1.refs_2_, f32[34,5,4,9,4,128]{5,4,3,2,1,0:T(4,128)} %bitcast.8), custom_call_target="tpu_custom_call" | custom-call | tf_op jit(solution)/shard_map/place/pallas_call | solution.py:680
  57.0 0.0 collective-permute-done.5.refs_1_
  57.0 0.0 collective-permute-done.6.refs_2_
  57.0 1.4 %more.2.refs_0_ = f32[30,6,3,8,128]{4,3,2,1,0:T(8,128)S(1)} custom-call(f32[30,6,3,8,128]{4,3,2,1,0:T(8,128)S(1)} %place.1.refs_0_, f32[544,128]{1,0:T(8,128)S(1)} %collective-permute-done.5.refs_1_, f32[544,128]{1,0:T(8,128)S(1)} %collective-permute-done.6.refs_2_, f32[34,5,4,9,4,128]{5,4,3,2,1,0:T(4,128)} %bitcast.9), custom_call_target="tpu_custom_call", output_to_operand_aliasing={{}: (0, {})} | custom-call | tf_op jit(solution)/shard_map/more/pallas_call | solution.py:748
  58.5 0.0 collective-permute-done.7.refs_1_
  58.5 6.3 %collective-permute-done.8.refs_2_ = f32[544,128]{1,0:T(8,128)S(1)} collective-permute-done((f32[544,128]{1,0:T(8,128)S(1)}, f32[544,128]{1,0:T(8,128)S(1)}, u32[]{:S(2)}, u32[]{:S(2)}) %collective-permute-start.8) | collective-permute-done | bytes 278560 | tf_op jit(solution)/shard_map/ppermute | solution.py:772
  64.8 1.3 %more.3.staged_ref = f32[30,6,3,8,128]{4,3,2,1,0:T(8,128)S(1)} custom-call(f32[30,6,3,8,128]{4,3,2,1,0:T(8,128)S(1)} %more.2.refs_0_, f32[544,128]{1,0:T(8,128)S(1)} %collective-permute-done.7.refs_1_, f32[544,128]{1,0:T(8,128)S(1)} %collective-permute-done.8.refs_2_, f32[34,5,4,9,4,128]{5,4,3,2,1,0:T(4,128)} %bitcast.10), custom_call_target="tpu_custom_call", output_to_operand_aliasing={{}: (0, {})} | custom-call | tf_op jit(solution)/shard_map/more/pallas_call | solution.py:748
  66.1 0.0 collective-permute-done.9.refs_0_
  66.1 2.0 %finish.1 = f32[60,6,4,384]{3,2,1,0:T(4,128)} custom-call(f32[30,6,3,8,128]{4,3,2,1,0:T(8,128)S(1)} %more.3.staged_ref, f32[544,128]{1,0:T(8,128)S(1)} %collective-permute-done.9.refs_0_), custom_call_target="tpu_custom_call" | custom-call | tf_op jit(solution)/shard_map/finish/pallas_call | solution.py:713
  (2 shorter events, 0.0 us)
Async XLA Ops:
  5.4 12.6 %collective-permute-start = (f32[40,256]{1,0:T(8,128)S(1)}, f32[40,256]{1,0:T(8,128)S(1)}, u32[]{:S(2)}, u32[]{:S(2)}) collective-permute-start(f32[40,256]{1,0:T(8,128)S(1)} %get-tuple-element.20.refs_5_.refs_1_), channel_id=1, source_target_pairs={{0,2},{2,4},{4,6},{6,8},{8,10},{10,12},{12,14},{14,0},{1,3},{3,5},... | collective-permute-start | bytes 122888 | tf_op jit(solution)/shard_map/ppermute | solution.py:778
  8.4 9.6 %collective-permute-start.1 = (f32[40,256]{1,0:T(8,128)S(1)}, f32[40,256]{1,0:T(8,128)S(1)}, u32[]{:S(2)}, u32[]{:S(2)}) collective-permute-start(f32[40,256]{1,0:T(8,128)S(1)} %get-tuple-element.19.refs_4_.refs_0_), channel_id=1, source_target_pairs={{2,0},{4,2},{6,4},{8,6},{10,8},{12,10},{14,12},{0,14},{3,1},{5,3},... | collective-permute-start | bytes 122888 | tf_op jit(solution)/shard_map/ppermute | solution.py:777
  11.5 6.5 %copy-start = (s32[1,8]{1,0:T(1,128)S(1)}, s32[1,8]{1,0:T(1,128)}, u32[]{:S(2)}) copy-start(s32[1,8]{1,0:T(1,128)} %owner_ref.9) | copy-start | bytes 100
  11.5 21.1 %collective-permute-start.3 = (f32[544,128]{1,0:T(8,128)S(1)}, f32[544,128]{1,0:T(8,128)S(1)}, u32[]{:S(2)}, u32[]{:S(2)}) collective-permute-start(f32[544,128]{1,0:T(8,128)S(1)} %get-tuple-element.25), channel_id=1, source_target_pairs={{0,8},{2,10},{4,12},{6,14},{8,0},{10,2},{12,4},{14,6},{1,9},{3,11}... | collective-permute-start | bytes 835592 | tf_op jit(solution)/shard_map/ppermute | solution.py:772
  20.7 31.7 %collective-permute-start.2 = (f32[544,128]{1,0:T(8,128)S(1)}, f32[544,128]{1,0:T(8,128)S(1)}, u32[]{:S(2)}, u32[]{:S(2)}) collective-permute-start(f32[544,128]{1,0:T(8,128)S(1)} %get-tuple-element.24.refs_0_), channel_id=1, source_target_pairs={{0,10},{2,8},{4,14},{6,12},{8,2},{10,0},{12,6},{14,4},{1,11},{3,9}... | collective-permute-start | bytes 835592 | tf_op jit(solution)/shard_map/ppermute | solution.py:772
  36.5 16.0 %collective-permute-start.4 = (f32[32,256]{1,0:T(8,128)S(1)}, f32[32,256]{1,0:T(8,128)S(1)}, u32[]{:S(2)}, u32[]{:S(2)}) collective-permute-start(f32[32,256]{1,0:T(8,128)S(1)} %get-tuple-element.29), channel_id=1, source_target_pairs={{0,8},{2,10},{4,12},{6,14},{8,0},{10,2},{12,4},{14,6},{1,9},{3,11}... | collective-permute-start | bytes 98312 | tf_op jit(solution)/shard_map/ppermute | solution.py:772
  36.5 20.5 %collective-permute-start.5 = (f32[544,128]{1,0:T(8,128)S(1)}, f32[544,128]{1,0:T(8,128)S(1)}, u32[]{:S(2)}, u32[]{:S(2)}) collective-permute-start(f32[544,128]{1,0:T(8,128)S(1)} %get-tuple-element.28.refs_1_), channel_id=1, source_target_pairs={{0,12},{2,14},{4,8},{6,10},{8,4},{10,6},{12,0},{14,2},{1,13},{3,15... | collective-permute-start | bytes 835592 | tf_op jit(solution)/shard_map/ppermute | solution.py:772
  38.6 18.4 %collective-permute-start.6 = (f32[544,128]{1,0:T(8,128)S(1)}, f32[544,128]{1,0:T(8,128)S(1)}, u32[]{:S(2)}, u32[]{:S(2)}) collective-permute-start(f32[544,128]{1,0:T(8,128)S(1)} %get-tuple-element.30), channel_id=1, source_target_pairs={{0,14},{2,12},{4,10},{6,8},{8,6},{10,4},{12,2},{14,0},{1,15},{3,13... | collective-permute-start | bytes 835592 | tf_op jit(solution)/shard_map/ppermute | solution.py:772
  41.8 16.6 %collective-permute-start.7 = (f32[544,128]{1,0:T(8,128)S(1)}, f32[544,128]{1,0:T(8,128)S(1)}, u32[]{:S(2)}, u32[]{:S(2)}) collective-permute-start(f32[544,128]{1,0:T(8,128)S(1)} %get-tuple-element.31.refs_0_), channel_id=1, source_target_pairs={{0,6},{2,4},{4,2},{6,0},{8,14},{10,12},{12,10},{14,8},{1,7},{3,5},... | collective-permute-start | bytes 835592 | tf_op jit(solution)/shard_map/ppermute | solution.py:772
  52.4 12.3 %collective-permute-start.8 = (f32[544,128]{1,0:T(8,128)S(1)}, f32[544,128]{1,0:T(8,128)S(1)}, u32[]{:S(2)}, u32[]{:S(2)}) collective-permute-start(f32[544,128]{1,0:T(8,128)S(1)} %get-tuple-element.32), channel_id=1, source_target_pairs={{0,4},{2,6},{4,0},{6,2},{8,12},{10,14},{12,8},{14,10},{1,5},{3,7},... | collective-permute-start | bytes 835592 | tf_op jit(solution)/shard_map/ppermute | solution.py:772
  52.4 13.7 %collective-permute-start.9 = (f32[544,128]{1,0:T(8,128)S(1)}, f32[544,128]{1,0:T(8,128)S(1)}, u32[]{:S(2)}, u32[]{:S(2)}) collective-permute-start(f32[544,128]{1,0:T(8,128)S(1)} %block_1.1), channel_id=1, source_target_pairs={{0,2},{2,0},{4,6},{6,4},{8,10},{10,8},{12,14},{14,12},{1,3},{3,1},... | collective-permute-start | bytes 835592 | tf_op jit(solution)/shard_map/ppermute | solution.py:772
where the time goes:
time: 68.5 us; the launch traced here: 68.3 us
  Pallas kernels  33.1 us (48%)
  waiting for transfers between devices  21.8 us (32%)
  starting transfers between devices  13.1 us (19%)
    ppermute x8, waiting for transfers between devices, send(): return lax.ppermute(value, 'tile', [(i, i ^ step) for i in range(tiles)])  21.8 us
    pallas_call x4, Pallas kernels, block_call(): pl.pallas_call(kernel, out_shape=outs, in_specs=[pl.BlockSpec(memory_spac...  12.4 us
    ppermute x8, starting transfers between devices, send(): return lax.ppermute(value, 'tile', [(i, i ^ step) for i in range(tiles)])  6.99 us
    pallas_call x1, Pallas kernels, fold_call(): pl.pallas_call(kernel, out_shape=[pltpu.VMEM((size.point_tiles, size.forc...  5.56 us
    pallas_call x1, Pallas kernels, first_call(): pl.pallas_call(kernel, out_shape=[pltpu.VMEM((size.packed, LANES), jnp.fl...  5.37 us
    ppermute x1, starting transfers between devices, shards(): from_right = lax.ppermute(edges[0], 'tile', down)  3.1 us
    ppermute x1, starting transfers between devices, shards(): from_left = lax.ppermute(edges[1], 'tile', up)  3.02 us
    pallas_call x2, Pallas kernels, more_call(): pl.pallas_call(kernel, out_shape=pltpu.VMEM(shape, jnp.float32), in_specs...  2.75 us
  transfers between devices with their start and end apart: 10, of which 3 were waited for; matrix products, arithmetic and copies ran while one was open for 0% of the time, Pallas kernels for 38%

commit v1 on v0

--- a/solution.py
+++ b/solution.py
@@ -16,8 +16,8 @@
 SPILL_ROWS = 32
 EDGE_ROWS = 40
 FAR = -(1 << 20)
-VMEM_BYTES = 53 << 20
-BLOCK_VMEM = 32 << 20
+VMEM_BYTES = 28 << 20
+BLOCK_VMEM = 16 << 20
 
 
 def zone_factors(forced):
@@ -562,8 +562,22 @@
     )(owner, *map(in_vmem, [*edges, from_left, from_right, parts, ints, floats]))
 
 
-def fix_call(size, block, fix):
-    def kernel(block_ref, fix_ref, out_ref):
+def hand_on(value, after):
+    def kernel(value_ref, *refs):
+        refs[-1][...] = value_ref[...]
+
+    vmem = pl.BlockSpec(memory_space=pltpu.VMEM)
+    return pl.pallas_call(
+        kernel,
+        out_shape=pltpu.VMEM(value.shape, jnp.float32),
+        in_specs=[vmem] * (1 + len(after)),
+        out_specs=vmem,
+        name="hand_on",
+    )(in_vmem(value), *map(in_vmem, after))
+
+
+def fix_call(size, block, fix, after):
+    def kernel(block_ref, fix_ref, _, out_ref):
         values = fix_ref[...]
         values = jnp.concatenate(
             [values, jnp.zeros((LANES - SPILL_ROWS, size.wide), jnp.float32)], axis=0
@@ -595,11 +609,11 @@
     return pl.pallas_call(
         kernel,
         out_shape=pltpu.VMEM((size.packed, LANES), jnp.float32),
-        in_specs=[vmem] * 2,
+        in_specs=[vmem] * 3,
         out_specs=vmem,
         compiler_params=pltpu.CompilerParams(vmem_limit_bytes=VMEM_BYTES),
         name="fix",
-    )(in_vmem(block), in_vmem(fix))
+    )(in_vmem(block), in_vmem(fix), in_vmem(after))
 
 
 def pieces(size, source, member):
@@ -781,22 +795,19 @@
         size, early, far[1], owner_map, edges, from_left, from_right, parts, ints, floats
     )
     arrived[far[1]] = send(far[1], block)
-    made = [block]
     turns = [kind[i : i + 2] for kind in (far[2:], near) for i in range(0, len(kind), 2)]
-    for turn in turns:
-        fixes = turn[0] == near[0]
-        after = list(made[:1]) + ([arrived[early]] if fixes else [])
-        made = block_call(size, turn, owner_map, parts, ints, floats, across, fix if fixes else None, after)
-        for step, block in zip(turn, made):
-            arrived[step] = send(step, block)
-        if fixes:
-            fix = send(early, made[-1])
-    arrived[0] = block_call(size, [0], owner_map, parts, ints, floats, across)[0]
-    arrived[early] = fix_call(size, arrived[early], fix)
-    staged = place_call(size, {step: arrived[step] for step in (far[1], early, 0)}, tiled)
+    made = block_call(size, far[2:] + near, owner_map, parts, ints, floats, across, None, [block])
+    for step, block in zip(far[2:] + near, made):
+        arrived[step] = send(step, block)
+    arrived[0] = block_call(
+        size, [0], owner_map, parts, ints, floats, across, None, [made[0], arrived[early]]
+    )[0]
+    fix = send(early, hand_on(fix, [arrived[0]]))
+    staged = place_call(size, {step: arrived[step] for step in (far[1], 0)}, tiled)
     for turn in turns[:-1]:
         staged = more_call(size, staged, {step: arrived[step] for step in turn}, tiled)
-    placed = finish_call(size, staged, {step: arrived[step] for step in turns[-1]})
+    arrived[early] = fix_call(size, arrived[early], fix, staged)
+    placed = finish_call(size, staged, {step: arrived[step] for step in turns[-1] + [early]})
     placed = placed.reshape(NT, size.fields, PROWS, size.levels, size.par)
     return jnp.transpose(placed, (0, 1, 3, 2, 4))
 

time: 68.5 us -> 66.6 us (0.972)
  the two profiles are of different devices: /device:TPU:0 before, /device:TPU:8 now
where the time goes in v1:
time: 66.6 us; the launch traced here: 66.4 us
  Pallas kernels  32.2 us (48%)
  waiting for transfers between devices  19.6 us (29%)
  starting transfers between devices  14.2 us (21%)
    ppermute x8, waiting for transfers between devices, send(): return lax.ppermute(value, 'tile', [(i, i ^ step) for i in range(tiles)])  19.6 us
    ppermute x8, starting transfers between devices, send(): return lax.ppermute(value, 'tile', [(i, i ^ step) for i in range(tiles)])  12.2 us
    pallas_call x2, Pallas kernels, block_call(): pl.pallas_call(kernel, out_shape=outs, in_specs=[pl.BlockSpec(memory_spac...  12 us
    pallas_call x1, Pallas kernels, fold_call(): pl.pallas_call(kernel, out_shape=[pltpu.VMEM((size.point_tiles, size.forc...  5.56 us
    pallas_call x1, Pallas kernels, first_call(): pl.pallas_call(kernel, out_shape=[pltpu.VMEM((size.packed, LANES), jnp.fl...  5.38 us
    pallas_call x2, Pallas kernels, more_call(): pl.pallas_call(kernel, out_shape=pltpu.VMEM(shape, jnp.float32), in_specs...  2.73 us
    pallas_call x1, Pallas kernels, join_call(): pl.pallas_call(kernel, out_shape=[pltpu.VMEM((2 * size.lead, LANES), jnp....  2.73 us
    pallas_call x1, Pallas kernels, finish_call(): pl.pallas_call(kernel, out_shape=jax.ShapeDtypeStruct(shape, jnp.float32)...  2.22 us
  transfers between devices with their start and end apart: 10, of which 3 were waited for; matrix products, arithmetic and copies ran while one was open for 0% of the time, Pallas kernels for 37%

profile of v1, /device:TPU:8, one launch (start us, length us, event | category | flops | bytes accessed | tf_op | source)
XLA Modules:
  0.0 66.4 jit_solution(908824860898845294)
XLA Ops:
  0.0 5.4 %block_4.1 = (f32[544,128]{1,0:T(8,128)S(1)}, f32[40,256]{1,0:T(8,128)S(1)}, f32[40,256]{1,0:T(8,128)S(1)}) custom-call(s32[1,8]{1,0:T(1,128)} %owner_ref.5, f32[34,5,4,9,4,128]{5,4,3,2,1,0:T(4,128)} %bitcast.6, s32[5,1152]{1,0:T(8,128)} %refs_0_.3, s32[5,1152]{1,0:T(8,128)} %refs_1_.3, f32[5,1152]{1,0:T(8,128)} %refs_2_.3, f32[5,1152]{1,0:T(8,128)} %refs_3_.3), custom_call_target="tpu_custom_call" | custom-call | tf_op jit(solution)/shard_map/block_4/pallas_call | solution.py:380
  5.4 1.5 %collective-permute-start.1 = (f32[40,256]{1,0:T(8,128)S(1)}, f32[40,256]{1,0:T(8,128)S(1)}, u32[]{:S(2)}, u32[]{:S(2)}) collective-permute-start(f32[40,256]{1,0:T(8,128)S(1)} %get-tuple-element.19.refs_4_.refs_0_), channel_id=1, source_target_pairs={{2,0},{4,2},{6,4},{8,6},{10,8},{12,10},{14,12},{0,14},{3,1},{5,3},... | collective-permute-start | bytes 122888 | tf_op jit(solution)/shard_map/ppermute | solution.py:791
  6.8 0.6 collective-permute-start
  7.5 0.0 copy-start
  7.5 2.6 %collective-permute-start.3 = (f32[544,128]{1,0:T(8,128)S(1)}, f32[544,128]{1,0:T(8,128)S(1)}, u32[]{:S(2)}, u32[]{:S(2)}) collective-permute-start(f32[544,128]{1,0:T(8,128)S(1)} %get-tuple-element.27), channel_id=1, source_target_pairs={{0,8},{2,10},{4,12},{6,14},{8,0},{10,2},{12,4},{14,6},{1,9},{3,11}... | collective-permute-start | bytes 835592 | tf_op jit(solution)/shard_map/ppermute | solution.py:786
  10.1 5.6 %fold.1 = (bf16[9,4,480,128]{3,2,1,0:T(8,128)(2,1)S(1)}, s32[2,5,1152]{2,1,0:T(8,128)S(1)}, f32[2,5,1152]{2,1,0:T(8,128)S(1)}) custom-call(f32[34,5,4,9,4,128]{5,4,3,2,1,0:T(4,128)} %bitcast.7, s32[5,1152]{1,0:T(8,128)} %refs_0_.3, s32[5,1152]{1,0:T(8,128)} %refs_1_.3, f32[5,1152]{1,0:T(8,128)} %refs_2_.3, f32[5,1152]{1,0:T(8,128)} %refs_3_.3, ...), custom_call_target="tpu_custom_call" | custom-call | tf_op jit(solution)/shard_map/fold/pallas_call | solution.py:489
  15.6 0.0 collective-permute-done.1.refs_3_
  15.6 0.0 collective-permute-done.refs_2_
  15.6 0.0 copy-done
  15.7 2.7 %join.1 = (bf16[480,128]{1,0:T(8,128)(2,1)S(1)}, f32[32,256]{1,0:T(8,128)S(1)}, f32[544,128]{1,0:T(8,128)S(1)}) custom-call(s32[1,8]{1,0:T(1,128)S(1)} %copy-done, f32[40,256]{1,0:T(8,128)S(1)} %get-tuple-element.19.refs_4_.refs_0_, f32[40,256]{1,0:T(8,128)S(1)} %get-tuple-element.20.refs_5_.refs_1_, f32[40,256]{1,0:T(8,128)S(1)} %collective-permute-done.refs_2_, ...), custom_call_target="tpu_custom_call" | custom-call | tf_op jit(solution)/shard_map/join/pallas_call | solution.py:550
  18.4 3.7 %collective-permute-start.2 = (f32[544,128]{1,0:T(8,128)S(1)}, f32[544,128]{1,0:T(8,128)S(1)}, u32[]{:S(2)}, u32[]{:S(2)}) collective-permute-start(f32[544,128]{1,0:T(8,128)S(1)} %get-tuple-element.24.refs_0_), channel_id=1, source_target_pairs={{0,10},{2,8},{4,14},{6,12},{8,2},{10,0},{12,6},{14,4},{1,11},{3,9}... | collective-permute-start | bytes 835592 | tf_op jit(solution)/shard_map/ppermute | solution.py:786
  22.1 9.6 %block_6_7_3_2_1.1 = (f32[544,128]{1,0:T(8,128)S(1)}, f32[544,128]{1,0:T(8,128)}, f32[544,128]{1,0:T(8,128)S(1)}, f32[544,128]{1,0:T(8,128)S(1)}, f32[544,128]{1,0:T(8,128)S(1)}) custom-call(s32[1,8]{1,0:T(1,128)S(1)} %copy-done, bf16[9,4,480,128]{3,2,1,0:T(8,128)(2,1)S(1)} %get-tuple-element.21.refs_4_.parts_ref, ...), custom_call_target="tpu_custom_call" | custom-call | tf_op jit(solution)/shard_map/block_6_7_3_2_1/pallas_call | solution.py:443
  31.7 0.7 %collective-permute-start.5 = (f32[544,128]{1,0:T(8,128)}, f32[544,128]{1,0:T(8,128)S(1)}, u32[]{:S(2)}, u32[]{:S(2)}) collective-permute-start(f32[544,128]{1,0:T(8,128)} %get-tuple-element.28), channel_id=1, source_target_pairs={{0,14},{2,12},{4,10},{6,8},{8,6},{10,4},{12,2},{14,0},{1,15},{3,13... | collective-permute-start | bytes 835592 | tf_op jit(solution)/shard_map/ppermute | solution.py:786
  32.5 4.5 %collective-permute-start.6 = (f32[544,128]{1,0:T(8,128)S(1)}, f32[544,128]{1,0:T(8,128)S(1)}, u32[]{:S(2)}, u32[]{:S(2)}) collective-permute-start(f32[544,128]{1,0:T(8,128)S(1)} %get-tuple-element.29), channel_id=1, source_target_pairs={{0,6},{2,4},{4,2},{6,0},{8,14},{10,12},{12,10},{14,8},{1,7},{3,5},... | collective-permute-start | bytes 835592 | tf_op jit(solution)/shard_map/ppermute | solution.py:786
  37.0 0.0 collective-permute-start.4
  37.0 0.0 collective-permute-done.3.refs_1_.block_ref
  37.0 0.6 collective-permute-start.7
  37.6 3.0 %collective-permute-done.2.refs_0_ = f32[544,128]{1,0:T(8,128)S(1)} collective-permute-done((f32[544,128]{1,0:T(8,128)S(1)}, f32[544,128]{1,0:T(8,128)S(1)}, u32[]{:S(2)}, u32[]{:S(2)}) %collective-permute-start.2) | collective-permute-done | bytes 278560 | tf_op jit(solution)/shard_map/ppermute | solution.py:786
  40.6 0.0 collective-permute-start.8
  40.6 2.3 %block_0.1.refs_1_.refs_0_ = f32[544,128]{1,0:T(8,128)S(1)} custom-call(s32[1,8]{1,0:T(1,128)S(1)} %copy-done, bf16[9,4,480,128]{3,2,1,0:T(8,128)(2,1)S(1)} %get-tuple-element.21.refs_4_.parts_ref, s32[2,5,1152]{2,1,0:T(8,128)S(1)} %get-tuple-element.22.refs_5_.ints, f32[2,5,1152]{2,1,0:T(8,128)S(1)} %get-tuple-element.23.refs_6_.floats, ...), custom_call_target="tpu_custom_call" | custom-call | tf_op jit(solution)/shard_map/block_0/pallas_call | solution.py:443
  43.0 12.6 %collective-permute-done.5.refs_2_ = f32[544,128]{1,0:T(8,128)S(1)} collective-permute-done((f32[544,128]{1,0:T(8,128)}, f32[544,128]{1,0:T(8,128)S(1)}, u32[]{:S(2)}, u32[]{:S(2)}) %collective-permute-start.5) | collective-permute-done | bytes 278560 | tf_op jit(solution)/shard_map/ppermute | solution.py:786
  55.6 0.0 collective-permute-start.9
  55.6 1.2 %place.1.refs_0_ = f32[30,6,3,8,128]{4,3,2,1,0:T(8,128)S(1)} custom-call(f32[544,128]{1,0:T(8,128)S(1)} %collective-permute-done.2.refs_0_, f32[544,128]{1,0:T(8,128)S(1)} %block_0.1.refs_1_.refs_0_, f32[34,5,4,9,4,128]{5,4,3,2,1,0:T(4,128)} %bitcast.8), custom_call_target="tpu_custom_call" | custom-call | tf_op jit(solution)/shard_map/place/pallas_call | solution.py:694
  56.8 4.0 %collective-permute-done.4.refs_1_ = f32[544,128]{1,0:T(8,128)S(1)} collective-permute-done((f32[544,128]{1,0:T(8,128)S(1)}, f32[544,128]{1,0:T(8,128)S(1)}, u32[]{:S(2)}, u32[]{:S(2)}) %collective-permute-start.4) | collective-permute-done | bytes 278560 | tf_op jit(solution)/shard_map/ppermute | solution.py:786
  60.8 1.4 %more.2.refs_0_ = f32[30,6,3,8,128]{4,3,2,1,0:T(8,128)S(1)} custom-call(f32[30,6,3,8,128]{4,3,2,1,0:T(8,128)S(1)} %place.1.refs_0_, f32[544,128]{1,0:T(8,128)S(1)} %collective-permute-done.4.refs_1_, f32[544,128]{1,0:T(8,128)S(1)} %collective-permute-done.5.refs_2_, f32[34,5,4,9,4,128]{5,4,3,2,1,0:T(4,128)} %bitcast.9), custom_call_target="tpu_custom_call", output_to_operand_aliasing={{}: (0, {})} | custom-call | tf_op jit(solution)/shard_map/more/pallas_call | solution.py:762
  62.2 0.0 collective-permute-done.6.refs_1_
  62.2 0.0 collective-permute-done.7.refs_2_
  62.2 1.4 %more.3._.staged_ref = f32[30,6,3,8,128]{4,3,2,1,0:T(8,128)S(1)} custom-call(f32[30,6,3,8,128]{4,3,2,1,0:T(8,128)S(1)} %more.2.refs_0_, f32[544,128]{1,0:T(8,128)S(1)} %collective-permute-done.6.refs_1_, f32[544,128]{1,0:T(8,128)S(1)} %collective-permute-done.7.refs_2_, f32[34,5,4,9,4,128]{5,4,3,2,1,0:T(4,128)} %bitcast.10), custom_call_target="tpu_custom_call", output_to_operand_aliasing={{}: (0, {})} | custom-call | tf_op jit(solution)/shard_map/more/pallas_call | solution.py:762
  63.6 0.0 collective-permute-done.9.fix_ref
  63.6 0.4 fix.1.refs_1_
  64.0 0.0 collective-permute-done.8.refs_0_
  64.0 2.2 %finish.1 = f32[60,6,4,384]{3,2,1,0:T(4,128)} custom-call(f32[30,6,3,8,128]{4,3,2,1,0:T(8,128)S(1)} %more.3._.staged_ref, f32[544,128]{1,0:T(8,128)S(1)} %collective-permute-done.8.refs_0_, f32[544,128]{1,0:T(8,128)S(1)} %fix.1.refs_1_), custom_call_target="tpu_custom_call" | custom-call | tf_op jit(solution)/shard_map/finish/pallas_call | solution.py:727
  (1 shorter events, 0.0 us)
Async XLA Ops:
  5.4 10.2 %collective-permute-start.1 = (f32[40,256]{1,0:T(8,128)S(1)}, f32[40,256]{1,0:T(8,128)S(1)}, u32[]{:S(2)}, u32[]{:S(2)}) collective-permute-start(f32[40,256]{1,0:T(8,128)S(1)} %get-tuple-element.19.refs_4_.refs_0_), channel_id=1, source_target_pairs={{2,0},{4,2},{6,4},{8,6},{10,8},{12,10},{14,12},{0,14},{3,1},{5,3},... | collective-permute-start | bytes 122888 | tf_op jit(solution)/shard_map/ppermute | solution.py:791
  6.8 8.8 %collective-permute-start = (f32[40,256]{1,0:T(8,128)S(1)}, f32[40,256]{1,0:T(8,128)S(1)}, u32[]{:S(2)}, u32[]{:S(2)}) collective-permute-start(f32[40,256]{1,0:T(8,128)S(1)} %get-tuple-element.20.refs_5_.refs_1_), channel_id=1, source_target_pairs={{0,2},{2,4},{4,6},{6,8},{8,10},{10,12},{12,14},{14,0},{1,3},{3,5},... | collective-permute-start | bytes 122888 | tf_op jit(solution)/shard_map/ppermute | solution.py:792
  7.5 8.2 %copy-start = (s32[1,8]{1,0:T(1,128)S(1)}, s32[1,8]{1,0:T(1,128)}, u32[]{:S(2)}) copy-start(s32[1,8]{1,0:T(1,128)} %owner_ref.5) | copy-start | bytes 100
  7.5 29.6 %collective-permute-start.3 = (f32[544,128]{1,0:T(8,128)S(1)}, f32[544,128]{1,0:T(8,128)S(1)}, u32[]{:S(2)}, u32[]{:S(2)}) collective-permute-start(f32[544,128]{1,0:T(8,128)S(1)} %get-tuple-element.27), channel_id=1, source_target_pairs={{0,8},{2,10},{4,12},{6,14},{8,0},{10,2},{12,4},{14,6},{1,9},{3,11}... | collective-permute-start | bytes 835592 | tf_op jit(solution)/shard_map/ppermute | solution.py:786
  18.4 22.2 %collective-permute-start.2 = (f32[544,128]{1,0:T(8,128)S(1)}, f32[544,128]{1,0:T(8,128)S(1)}, u32[]{:S(2)}, u32[]{:S(2)}) collective-permute-start(f32[544,128]{1,0:T(8,128)S(1)} %get-tuple-element.24.refs_0_), channel_id=1, source_target_pairs={{0,10},{2,8},{4,14},{6,12},{8,2},{10,0},{12,6},{14,4},{1,11},{3,9}... | collective-permute-start | bytes 835592 | tf_op jit(solution)/shard_map/ppermute | solution.py:786
  31.7 23.8 %collective-permute-start.5 = (f32[544,128]{1,0:T(8,128)}, f32[544,128]{1,0:T(8,128)S(1)}, u32[]{:S(2)}, u32[]{:S(2)}) collective-permute-start(f32[544,128]{1,0:T(8,128)} %get-tuple-element.28), channel_id=1, source_target_pairs={{0,14},{2,12},{4,10},{6,8},{8,6},{10,4},{12,2},{14,0},{1,15},{3,13... | collective-permute-start | bytes 835592 | tf_op jit(solution)/shard_map/ppermute | solution.py:786
  32.5 29.7 %collective-permute-start.6 = (f32[544,128]{1,0:T(8,128)S(1)}, f32[544,128]{1,0:T(8,128)S(1)}, u32[]{:S(2)}, u32[]{:S(2)}) collective-permute-start(f32[544,128]{1,0:T(8,128)S(1)} %get-tuple-element.29), channel_id=1, source_target_pairs={{0,6},{2,4},{4,2},{6,0},{8,14},{10,12},{12,10},{14,8},{1,7},{3,5},... | collective-permute-start | bytes 835592 | tf_op jit(solution)/shard_map/ppermute | solution.py:786
  37.0 23.8 %collective-permute-start.4 = (f32[544,128]{1,0:T(8,128)S(1)}, f32[544,128]{1,0:T(8,128)S(1)}, u32[]{:S(2)}, u32[]{:S(2)}) collective-permute-start(f32[544,128]{1,0:T(8,128)S(1)} %get-tuple-element.26.refs_0_), channel_id=1, source_target_pairs={{0,12},{2,14},{4,8},{6,10},{8,4},{10,6},{12,0},{14,2},{1,13},{3,15... | collective-permute-start | bytes 835592 | tf_op jit(solution)/shard_map/ppermute | solution.py:786
  37.0 25.1 %collective-permute-start.7 = (f32[544,128]{1,0:T(8,128)S(1)}, f32[544,128]{1,0:T(8,128)S(1)}, u32[]{:S(2)}, u32[]{:S(2)}) collective-permute-start(f32[544,128]{1,0:T(8,128)S(1)} %get-tuple-element.30), channel_id=1, source_target_pairs={{0,4},{2,6},{4,0},{6,2},{8,12},{10,14},{12,8},{14,10},{1,5},{3,7},... | collective-permute-start | bytes 835592 | tf_op jit(solution)/shard_map/ppermute | solution.py:786
  40.6 23.3 %collective-permute-start.8 = (f32[544,128]{1,0:T(8,128)S(1)}, f32[544,128]{1,0:T(8,128)S(1)}, u32[]{:S(2)}, u32[]{:S(2)}) collective-permute-start(f32[544,128]{1,0:T(8,128)S(1)} %get-tuple-element.31), channel_id=1, source_target_pairs={{0,2},{2,0},{4,6},{6,4},{8,10},{10,8},{12,14},{14,12},{1,3},{3,1},... | collective-permute-start | bytes 835592 | tf_op jit(solution)/shard_map/ppermute | solution.py:786
  55.6 8.0 %collective-permute-start.9 = (f32[32,256]{1,0:T(8,128)S(1)}, f32[32,256]{1,0:T(8,128)S(1)}, u32[]{:S(2)}, u32[]{:S(2)}) collective-permute-start(f32[32,256]{1,0:T(8,128)S(1)} %hand_on.1), channel_id=1, source_target_pairs={{0,8},{2,10},{4,12},{6,14},{8,0},{10,2},{12,4},{14,6},{1,9},{3,11}... | collective-permute-start | bytes 98312 | tf_op jit(solution)/shard_map/ppermute | solution.py:786

commit v2 on v1

--- a/solution.py
+++ b/solution.py
@@ -297,6 +297,7 @@
             copies.append(copy)
         for copy in point_copies:
             copy.wait()
+        block_stencil(size, me, block, first_tile, ints, floats, right_hi, right_lo)
         center, diffuse = zone_factors(size.forced)
         lane = lax.broadcasted_iota(jnp.int32, (zone, LANES), 1)
         entry = lax.broadcasted_iota(jnp.int32, (SPILL_ROWS, LANES), 0)
@@ -355,7 +356,6 @@
                     value = (ints if kind < 2 else floats)[kind % 2, row : row + 1, point : point + 1]
                     edge_ref[start : start + 1] = jnp.broadcast_to(value.astype(jnp.float32), (1, size.wide))
                     start += 1
-        block_stencil(size, me, block, first_tile, ints, floats, right_hi, right_lo)
         pieces = []
         for first, last in chunks:
             for field in range(first, last):
@@ -541,7 +541,8 @@
         fixed = block_of(size, owner_ref, me ^ early)
         fix = jnp.where(fixed == 0, spills[0], jnp.where(fixed == size.tiles - 1, spills[1], 0.0))
         flag = jnp.where(fixed == 0, 1.0, 0.0)
-        fix_ref[...] = jnp.where(entry == SPILL_ROWS - 1, flag, fix)
+        lane = lax.broadcasted_iota(jnp.int32, fix.shape, 1)
+        fix_ref[...] = jnp.where(lane == size.wide - 1, flag, fix)[: PROWS * SPILL]
         write_blocks(
             size, [step], owner_ref, parts_ref, ints, floats, across_ref, [out_ref], right_hi, right_lo
         )
@@ -551,7 +552,7 @@
         kernel,
         out_shape=[
             pltpu.VMEM((2 * size.lead, LANES), jnp.bfloat16),
-            pltpu.VMEM((SPILL_ROWS, size.wide), jnp.float32),
+            pltpu.VMEM((PROWS * SPILL, size.wide), jnp.float32),
             pltpu.VMEM((size.packed, LANES), jnp.float32),
         ],
         in_specs=[pl.BlockSpec(memory_space=pltpu.SMEM)] + [vmem] * 7,
@@ -580,10 +581,10 @@
     def kernel(block_ref, fix_ref, _, out_ref):
         values = fix_ref[...]
         values = jnp.concatenate(
-            [values, jnp.zeros((LANES - SPILL_ROWS, size.wide), jnp.float32)], axis=0
+            [values, jnp.zeros((LANES - PROWS * SPILL, size.wide), jnp.float32)], axis=0
         )
         across = jnp.transpose(values)[: size.lead]
-        at_left = fix_ref[SPILL_ROWS - 1, 0] > 0.5
+        at_left = fix_ref[0, size.wide - 1] > 0.5
         column = lax.broadcasted_iota(jnp.int32, (size.cols, LANES), 0)
         entry = lax.broadcasted_iota(jnp.int32, (size.cols, LANES), 1)
         hits = [

time: 66.6 us -> 66.2 us (level)
  no operation moved by 1% of the time
where the time goes in v2:
time: 66.2 us; the launch traced here: 65.9 us
  Pallas kernels  32 us (48%)
  waiting for transfers between devices  19.4 us (29%)
  starting transfers between devices  14.2 us (21%)
    ppermute x8, waiting for transfers between devices, send(): return lax.ppermute(value, 'tile', [(i, i ^ step) for i in range(tiles)])  19.4 us
    ppermute x8, starting transfers between devices, send(): return lax.ppermute(value, 'tile', [(i, i ^ step) for i in range(tiles)])  12.2 us
    pallas_call x2, Pallas kernels, block_call(): pl.pallas_call(kernel, out_shape=outs, in_specs=[pl.BlockSpec(memory_spac...  12 us
    pallas_call x1, Pallas kernels, fold_call(): pl.pallas_call(kernel, out_shape=[pltpu.VMEM((size.point_tiles, size.forc...  5.56 us
    pallas_call x1, Pallas kernels, first_call(): pl.pallas_call(kernel, out_shape=[pltpu.VMEM((size.packed, LANES), jnp.fl...  5.1 us
    pallas_call x2, Pallas kernels, more_call(): pl.pallas_call(kernel, out_shape=pltpu.VMEM(shape, jnp.float32), in_specs...  2.73 us
    pallas_call x1, Pallas kernels, join_call(): pl.pallas_call(kernel, out_shape=[pltpu.VMEM((2 * size.lead, LANES), jnp....  2.73 us
    pallas_call x1, Pallas kernels, finish_call(): pl.pallas_call(kernel, out_shape=jax.ShapeDtypeStruct(shape, jnp.float32)...  2.22 us
  transfers between devices with their start and end apart: 10, of which 3 were waited for; matrix products, arithmetic and copies ran while one was open for 0% of the time, Pallas kernels for 37%

profile of v2, /device:TPU:8, one launch (start us, length us, event | category | flops | bytes accessed | tf_op | source)
XLA Modules:
  0.0 65.9 jit_solution(7146309195122515076)
XLA Ops:
  0.0 5.1 %block_4.1 = (f32[544,128]{1,0:T(8,128)S(1)}, f32[40,256]{1,0:T(8,128)S(1)}, f32[40,256]{1,0:T(8,128)S(1)}) custom-call(s32[1,8]{1,0:T(1,128)} %owner_ref.5, f32[34,5,4,9,4,128]{5,4,3,2,1,0:T(4,128)} %bitcast.6, s32[5,1152]{1,0:T(8,128)} %refs_0_.3, s32[5,1152]{1,0:T(8,128)} %refs_1_.3, f32[5,1152]{1,0:T(8,128)} %refs_2_.3, f32[5,1152]{1,0:T(8,128)} %refs_3_.3), custom_call_target="tpu_custom_call" | custom-call | tf_op jit(solution)/shard_map/block_4/pallas_call | solution.py:380
  5.1 1.5 %collective-permute-start.1 = (f32[40,256]{1,0:T(8,128)S(1)}, f32[40,256]{1,0:T(8,128)S(1)}, u32[]{:S(2)}, u32[]{:S(2)}) collective-permute-start(f32[40,256]{1,0:T(8,128)S(1)} %get-tuple-element.19.refs_4_.refs_0_), channel_id=1, source_target_pairs={{2,0},{4,2},{6,4},{8,6},{10,8},{12,10},{14,12},{0,14},{3,1},{5,3},... | collective-permute-start | bytes 122888 | tf_op jit(solution)/shard_map/ppermute | solution.py:792
  6.6 0.6 collective-permute-start
  7.2 0.0 copy-start
  7.2 2.6 %collective-permute-start.3 = (f32[544,128]{1,0:T(8,128)S(1)}, f32[544,128]{1,0:T(8,128)S(1)}, u32[]{:S(2)}, u32[]{:S(2)}) collective-permute-start(f32[544,128]{1,0:T(8,128)S(1)} %get-tuple-element.27), channel_id=1, source_target_pairs={{0,8},{2,10},{4,12},{6,14},{8,0},{10,2},{12,4},{14,6},{1,9},{3,11}... | collective-permute-start | bytes 835592 | tf_op jit(solution)/shard_map/ppermute | solution.py:787
  9.8 5.6 %fold.1 = (bf16[9,4,480,128]{3,2,1,0:T(8,128)(2,1)S(1)}, s32[2,5,1152]{2,1,0:T(8,128)S(1)}, f32[2,5,1152]{2,1,0:T(8,128)S(1)}) custom-call(f32[34,5,4,9,4,128]{5,4,3,2,1,0:T(4,128)} %bitcast.7, s32[5,1152]{1,0:T(8,128)} %refs_0_.3, s32[5,1152]{1,0:T(8,128)} %refs_1_.3, f32[5,1152]{1,0:T(8,128)} %refs_2_.3, f32[5,1152]{1,0:T(8,128)} %refs_3_.3, ...), custom_call_target="tpu_custom_call" | custom-call | tf_op jit(solution)/shard_map/fold/pallas_call | solution.py:489
  15.4 0.0 collective-permute-done.1.refs_3_
  15.4 0.0 collective-permute-done.refs_2_
  15.4 0.0 copy-done
  15.4 2.7 %join.1 = (bf16[480,128]{1,0:T(8,128)(2,1)S(1)}, f32[24,256]{1,0:T(8,128)S(1)}, f32[544,128]{1,0:T(8,128)S(1)}) custom-call(s32[1,8]{1,0:T(1,128)S(1)} %copy-done, f32[40,256]{1,0:T(8,128)S(1)} %get-tuple-element.19.refs_4_.refs_0_, f32[40,256]{1,0:T(8,128)S(1)} %get-tuple-element.20.refs_5_.refs_1_, f32[40,256]{1,0:T(8,128)S(1)} %collective-permute-done.refs_2_, ...), custom_call_target="tpu_custom_call" | custom-call | tf_op jit(solution)/shard_map/join/pallas_call | solution.py:551
  18.1 3.7 %collective-permute-start.2 = (f32[544,128]{1,0:T(8,128)S(1)}, f32[544,128]{1,0:T(8,128)S(1)}, u32[]{:S(2)}, u32[]{:S(2)}) collective-permute-start(f32[544,128]{1,0:T(8,128)S(1)} %get-tuple-element.24.refs_0_), channel_id=1, source_target_pairs={{0,10},{2,8},{4,14},{6,12},{8,2},{10,0},{12,6},{14,4},{1,11},{3,9}... | collective-permute-start | bytes 835592 | tf_op jit(solution)/shard_map/ppermute | solution.py:787
  21.8 9.6 %block_6_7_3_2_1.1 = (f32[544,128]{1,0:T(8,128)S(1)}, f32[544,128]{1,0:T(8,128)}, f32[544,128]{1,0:T(8,128)S(1)}, f32[544,128]{1,0:T(8,128)S(1)}, f32[544,128]{1,0:T(8,128)S(1)}) custom-call(s32[1,8]{1,0:T(1,128)S(1)} %copy-done, bf16[9,4,480,128]{3,2,1,0:T(8,128)(2,1)S(1)} %get-tuple-element.21.refs_4_.parts_ref, ...), custom_call_target="tpu_custom_call" | custom-call | tf_op jit(solution)/shard_map/block_6_7_3_2_1/pallas_call | solution.py:443
  31.5 0.7 %collective-permute-start.5 = (f32[544,128]{1,0:T(8,128)}, f32[544,128]{1,0:T(8,128)S(1)}, u32[]{:S(2)}, u32[]{:S(2)}) collective-permute-start(f32[544,128]{1,0:T(8,128)} %get-tuple-element.28), channel_id=1, source_target_pairs={{0,14},{2,12},{4,10},{6,8},{8,6},{10,4},{12,2},{14,0},{1,15},{3,13... | collective-permute-start | bytes 835592 | tf_op jit(solution)/shard_map/ppermute | solution.py:787
  32.2 4.5 %collective-permute-start.6 = (f32[544,128]{1,0:T(8,128)S(1)}, f32[544,128]{1,0:T(8,128)S(1)}, u32[]{:S(2)}, u32[]{:S(2)}) collective-permute-start(f32[544,128]{1,0:T(8,128)S(1)} %get-tuple-element.29), channel_id=1, source_target_pairs={{0,6},{2,4},{4,2},{6,0},{8,14},{10,12},{12,10},{14,8},{1,7},{3,5},... | collective-permute-start | bytes 835592 | tf_op jit(solution)/shard_map/ppermute | solution.py:787
  36.8 0.0 collective-permute-start.4
  36.8 0.0 collective-permute-done.3.refs_1_.block_ref
  36.8 0.6 collective-permute-start.7
  37.3 3.0 %collective-permute-done.2.refs_0_ = f32[544,128]{1,0:T(8,128)S(1)} collective-permute-done((f32[544,128]{1,0:T(8,128)S(1)}, f32[544,128]{1,0:T(8,128)S(1)}, u32[]{:S(2)}, u32[]{:S(2)}) %collective-permute-start.2) | collective-permute-done | bytes 278560 | tf_op jit(solution)/shard_map/ppermute | solution.py:787
  40.3 0.0 collective-permute-start.8
  40.3 2.3 %block_0.1.refs_1_.refs_0_ = f32[544,128]{1,0:T(8,128)S(1)} custom-call(s32[1,8]{1,0:T(1,128)S(1)} %copy-done, bf16[9,4,480,128]{3,2,1,0:T(8,128)(2,1)S(1)} %get-tuple-element.21.refs_4_.parts_ref, s32[2,5,1152]{2,1,0:T(8,128)S(1)} %get-tuple-element.22.refs_5_.ints, f32[2,5,1152]{2,1,0:T(8,128)S(1)} %get-tuple-element.23.refs_6_.floats, ...), custom_call_target="tpu_custom_call" | custom-call | tf_op jit(solution)/shard_map/block_0/pallas_call | solution.py:443
  42.7 12.6 %collective-permute-done.5.refs_2_ = f32[544,128]{1,0:T(8,128)S(1)} collective-permute-done((f32[544,128]{1,0:T(8,128)}, f32[544,128]{1,0:T(8,128)S(1)}, u32[]{:S(2)}, u32[]{:S(2)}) %collective-permute-start.5) | collective-permute-done | bytes 278560 | tf_op jit(solution)/shard_map/ppermute | solution.py:787
  55.3 0.0 collective-permute-start.9
  55.3 1.2 %place.1.refs_0_ = f32[30,6,3,8,128]{4,3,2,1,0:T(8,128)S(1)} custom-call(f32[544,128]{1,0:T(8,128)S(1)} %collective-permute-done.2.refs_0_, f32[544,128]{1,0:T(8,128)S(1)} %block_0.1.refs_1_.refs_0_, f32[34,5,4,9,4,128]{5,4,3,2,1,0:T(4,128)} %bitcast.8), custom_call_target="tpu_custom_call" | custom-call | tf_op jit(solution)/shard_map/place/pallas_call | solution.py:695
  56.5 3.7 %collective-permute-done.4.refs_1_ = f32[544,128]{1,0:T(8,128)S(1)} collective-permute-done((f32[544,128]{1,0:T(8,128)S(1)}, f32[544,128]{1,0:T(8,128)S(1)}, u32[]{:S(2)}, u32[]{:S(2)}) %collective-permute-start.4) | collective-permute-done | bytes 278560 | tf_op jit(solution)/shard_map/ppermute | solution.py:787
  60.3 1.4 %more.2.refs_0_ = f32[30,6,3,8,128]{4,3,2,1,0:T(8,128)S(1)} custom-call(f32[30,6,3,8,128]{4,3,2,1,0:T(8,128)S(1)} %place.1.refs_0_, f32[544,128]{1,0:T(8,128)S(1)} %collective-permute-done.4.refs_1_, f32[544,128]{1,0:T(8,128)S(1)} %collective-permute-done.5.refs_2_, f32[34,5,4,9,4,128]{5,4,3,2,1,0:T(4,128)} %bitcast.9), custom_call_target="tpu_custom_call", output_to_operand_aliasing={{}: (0, {})} | custom-call | tf_op jit(solution)/shard_map/more/pallas_call | solution.py:763
  61.7 0.0 collective-permute-done.6.refs_1_
  61.7 0.0 collective-permute-done.7.refs_2_
  61.7 1.4 %more.3._.staged_ref = f32[30,6,3,8,128]{4,3,2,1,0:T(8,128)S(1)} custom-call(f32[30,6,3,8,128]{4,3,2,1,0:T(8,128)S(1)} %more.2.refs_0_, f32[544,128]{1,0:T(8,128)S(1)} %collective-permute-done.6.refs_1_, f32[544,128]{1,0:T(8,128)S(1)} %collective-permute-done.7.refs_2_, f32[34,5,4,9,4,128]{5,4,3,2,1,0:T(4,128)} %bitcast.10), custom_call_target="tpu_custom_call", output_to_operand_aliasing={{}: (0, {})} | custom-call | tf_op jit(solution)/shard_map/more/pallas_call | solution.py:763
  63.0 0.0 collective-permute-done.9.fix_ref
  63.1 0.4 fix.1.refs_1_
  63.5 0.0 collective-permute-done.8.refs_0_
  63.5 2.2 %finish.1 = f32[60,6,4,384]{3,2,1,0:T(4,128)} custom-call(f32[30,6,3,8,128]{4,3,2,1,0:T(8,128)S(1)} %more.3._.staged_ref, f32[544,128]{1,0:T(8,128)S(1)} %collective-permute-done.8.refs_0_, f32[544,128]{1,0:T(8,128)S(1)} %fix.1.refs_1_), custom_call_target="tpu_custom_call" | custom-call | tf_op jit(solution)/shard_map/finish/pallas_call | solution.py:728
  (1 shorter events, 0.0 us)
Async XLA Ops:
  5.1 10.2 %collective-permute-start.1 = (f32[40,256]{1,0:T(8,128)S(1)}, f32[40,256]{1,0:T(8,128)S(1)}, u32[]{:S(2)}, u32[]{:S(2)}) collective-permute-start(f32[40,256]{1,0:T(8,128)S(1)} %get-tuple-element.19.refs_4_.refs_0_), channel_id=1, source_target_pairs={{2,0},{4,2},{6,4},{8,6},{10,8},{12,10},{14,12},{0,14},{3,1},{5,3},... | collective-permute-start | bytes 122888 | tf_op jit(solution)/shard_map/ppermute | solution.py:792
  6.6 8.8 %collective-permute-start = (f32[40,256]{1,0:T(8,128)S(1)}, f32[40,256]{1,0:T(8,128)S(1)}, u32[]{:S(2)}, u32[]{:S(2)}) collective-permute-start(f32[40,256]{1,0:T(8,128)S(1)} %get-tuple-element.20.refs_5_.refs_1_), channel_id=1, source_target_pairs={{0,2},{2,4},{4,6},{6,8},{8,10},{10,12},{12,14},{14,0},{1,3},{3,5},... | collective-permute-start | bytes 122888 | tf_op jit(solution)/shard_map/ppermute | solution.py:793
  7.2 8.2 %copy-start = (s32[1,8]{1,0:T(1,128)S(1)}, s32[1,8]{1,0:T(1,128)}, u32[]{:S(2)}) copy-start(s32[1,8]{1,0:T(1,128)} %owner_ref.5) | copy-start | bytes 100
  7.2 29.6 %collective-permute-start.3 = (f32[544,128]{1,0:T(8,128)S(1)}, f32[544,128]{1,0:T(8,128)S(1)}, u32[]{:S(2)}, u32[]{:S(2)}) collective-permute-start(f32[544,128]{1,0:T(8,128)S(1)} %get-tuple-element.27), channel_id=1, source_target_pairs={{0,8},{2,10},{4,12},{6,14},{8,0},{10,2},{12,4},{14,6},{1,9},{3,11}... | collective-permute-start | bytes 835592 | tf_op jit(solution)/shard_map/ppermute | solution.py:787
  18.1 22.2 %collective-permute-start.2 = (f32[544,128]{1,0:T(8,128)S(1)}, f32[544,128]{1,0:T(8,128)S(1)}, u32[]{:S(2)}, u32[]{:S(2)}) collective-permute-start(f32[544,128]{1,0:T(8,128)S(1)} %get-tuple-element.24.refs_0_), channel_id=1, source_target_pairs={{0,10},{2,8},{4,14},{6,12},{8,2},{10,0},{12,6},{14,4},{1,11},{3,9}... | collective-permute-start | bytes 835592 | tf_op jit(solution)/shard_map/ppermute | solution.py:787
  31.5 23.8 %collective-permute-start.5 = (f32[544,128]{1,0:T(8,128)}, f32[544,128]{1,0:T(8,128)S(1)}, u32[]{:S(2)}, u32[]{:S(2)}) collective-permute-start(f32[544,128]{1,0:T(8,128)} %get-tuple-element.28), channel_id=1, source_target_pairs={{0,14},{2,12},{4,10},{6,8},{8,6},{10,4},{12,2},{14,0},{1,15},{3,13... | collective-permute-start | bytes 835592 | tf_op jit(solution)/shard_map/ppermute | solution.py:787
  32.2 29.4 %collective-permute-start.6 = (f32[544,128]{1,0:T(8,128)S(1)}, f32[544,128]{1,0:T(8,128)S(1)}, u32[]{:S(2)}, u32[]{:S(2)}) collective-permute-start(f32[544,128]{1,0:T(8,128)S(1)} %get-tuple-element.29), channel_id=1, source_target_pairs={{0,6},{2,4},{4,2},{6,0},{8,14},{10,12},{12,10},{14,8},{1,7},{3,5},... | collective-permute-start | bytes 835592 | tf_op jit(solution)/shard_map/ppermute | solution.py:787
  36.8 23.5 %collective-permute-start.4 = (f32[544,128]{1,0:T(8,128)S(1)}, f32[544,128]{1,0:T(8,128)S(1)}, u32[]{:S(2)}, u32[]{:S(2)}) collective-permute-start(f32[544,128]{1,0:T(8,128)S(1)} %get-tuple-element.26.refs_0_), channel_id=1, source_target_pairs={{0,12},{2,14},{4,8},{6,10},{8,4},{10,6},{12,0},{14,2},{1,13},{3,15... | collective-permute-start | bytes 835592 | tf_op jit(solution)/shard_map/ppermute | solution.py:787
  36.8 24.9 %collective-permute-start.7 = (f32[544,128]{1,0:T(8,128)S(1)}, f32[544,128]{1,0:T(8,128)S(1)}, u32[]{:S(2)}, u32[]{:S(2)}) collective-permute-start(f32[544,128]{1,0:T(8,128)S(1)} %get-tuple-element.30), channel_id=1, source_target_pairs={{0,4},{2,6},{4,0},{6,2},{8,12},{10,14},{12,8},{14,10},{1,5},{3,7},... | collective-permute-start | bytes 835592 | tf_op jit(solution)/shard_map/ppermute | solution.py:787
  40.3 23.2 %collective-permute-start.8 = (f32[544,128]{1,0:T(8,128)S(1)}, f32[544,128]{1,0:T(8,128)S(1)}, u32[]{:S(2)}, u32[]{:S(2)}) collective-permute-start(f32[544,128]{1,0:T(8,128)S(1)} %get-tuple-element.31), channel_id=1, source_target_pairs={{0,2},{2,0},{4,6},{6,4},{8,10},{10,8},{12,14},{14,12},{1,3},{3,1},... | collective-permute-start | bytes 835592 | tf_op jit(solution)/shard_map/ppermute | solution.py:787
  55.3 7.8 %collective-permute-start.9 = (f32[24,256]{1,0:T(8,128)S(1)}, f32[24,256]{1,0:T(8,128)S(1)}, u32[]{:S(2)}, u32[]{:S(2)}) collective-permute-start(f32[24,256]{1,0:T(8,128)S(1)} %hand_on.1), channel_id=1, source_target_pairs={{0,8},{2,10},{4,12},{6,14},{8,0},{10,2},{12,4},{14,6},{1,9},{3,11}... | collective-permute-start | bytes 73736 | tf_op jit(solution)/shard_map/ppermute | solution.py:787
